TPU v7x, 512 devices: a whole 4x4x16 slice. The times are simulated.
512 devices in a mesh: dp: 4 (over x), vocab: 128 (over z, y, core).
Axes of the slice: x: 4, y: 4, z: 16, core: 2. Of those that a mesh axis runs over, the one named last changes fastest.
Arguments:
- hidden_states: bfloat16 [512, 4096], P('dp', 'vocab'), may hold values from -6 to 6
- teacher_logprob: bfloat16 [512, 131072], P(('dp', 'vocab')), may hold values from -12 to -0.5
- head_weight: bfloat16 [4096, 131072], P('dp', 'vocab'), may hold values from -6 to 6
- token_ids: int32 [512], P('dp'), may hold values from 0 to 131071
- padding_mask: int32 [512], P('dp'), may hold values 0 or 1
Outputs:
- logit_grad: bfloat16 [512, 131072], P('dp', 'vocab')
- hidden_grad: float32 [512, 4096], P('dp', 'vocab')
- head_grad: bfloat16 [4096, 131072], P('dp', 'vocab')
All inputs are finite; a program needn't handle non-finite values. No bound on the sum of `padding_mask` on one device may be relied on, other than what follows from the above.
Results may differ from a plain program's by a relative error of at most 0.012.
Values may be sent and summed in bfloat16 or wider, within the bound.
No kernel may reach another device: no remote copies, remote signals or barrier semaphores. Data moves between devices by JAX's collectives and lax.ppermute only.
A program may use at most 64 MiB of HBM per device.

v0:
```python
import jax
import jax.numpy as jnp
from jax import lax
from jax.sharding import PartitionSpec as P

anchor_weight = 0.25


def local(hidden_states, teacher_logprob, head_weight, token_ids, padding_mask):
    vocab_local = head_weight.shape[1]
    hidden_full = lax.all_gather(hidden_states, "vocab", axis=1, tiled=True)
    hidden_block = lax.all_to_all(hidden_full, "dp", split_axis=1, concat_axis=0, tiled=True)
    teacher = lax.all_to_all(teacher_logprob, "vocab", split_axis=1, concat_axis=0, tiled=True)
    head_full = lax.all_gather(head_weight, "dp", axis=0, tiled=True)
    logits = jnp.dot(hidden_full, head_full, preferred_element_type=jnp.float32)
    gap = logits - teacher.astype(jnp.float32)
    top = lax.pmax(jnp.max(logits, axis=1), "vocab")
    expo = jnp.exp(logits - top[:, None])
    total, weighted = lax.psum((jnp.sum(expo, axis=1), jnp.sum(expo * gap, axis=1)), "vocab")
    columns = lax.axis_index("vocab") * vocab_local + jnp.arange(vocab_local, dtype=jnp.int32)
    onehot = (columns[None, :] == token_ids[:, None]).astype(jnp.float32)
    prob = expo / total[:, None]
    keep = padding_mask.astype(jnp.float32)[:, None]
    logit_grad = (
        keep * (prob * (gap - (weighted / total)[:, None]) + anchor_weight * (prob - onehot))
    ).astype(jnp.bfloat16)
    head_grad = lax.dot_general(
        hidden_block,
        lax.all_gather(logit_grad, "dp", axis=0, tiled=True),
        (((0,), (0,)), ((), ())),
        preferred_element_type=jnp.float32,
    )
    feature_part = lax.dot_general(
        logit_grad, head_full, (((1,), (1,)), ((), ())), preferred_element_type=jnp.float32
    )
    hidden_grad = lax.psum_scatter(feature_part, "vocab", scatter_dimension=1, tiled=True)
    return (logit_grad, hidden_grad, head_grad.astype(jnp.bfloat16))


def solution(mesh):
    in_specs = (P("dp", "vocab"), P(("dp", "vocab"), None), P("dp", "vocab"), P("dp"), P("dp"))
    out_specs = (P("dp", "vocab"), P("dp", "vocab"), P("dp", "vocab"))
    return jax.shard_map(local, mesh=mesh, in_specs=in_specs, out_specs=out_specs, check_vma=False)
```

profile of v0, /device:TPU:6, one launch (start us, length us, event | category | flops | bytes accessed | tf_op | source)
XLA Modules:
  0.0 1044.4 jit_solution(5004442019393945415)
XLA Ops:
  7.2 0.7 all-gather.4.cloned.1.call-update
  7.9 0.7 all-gather.6.cloned.1.call-update
  8.6 0.5 broadcast.9
  9.2 3.1 reduce
  12.3 0.9 reshape.27
  13.2 20.0 %all-to-all-start = ((bf16[128,2,512]{2,1,0:T(2,128)(2,1)}), bf16[128,2,512]{2,1,0:T(2,128)(2,1)S(1)}, u32[]{:S(2)}, u32[]{:S(2)}) async-start(bf16[128,2,512]{2,1,0:T(2,128)(2,1)} %reshape.27), calls=%async_computation | async-start | bytes 524288 | tf_op jit(solution)/shard_map/all_to_all | solution.py:13
  33.1 0.0 all-gather.8.cloned.1.call-start
  33.2 0.7 convert_element_type.21
  33.9 19.5 %all-to-all-done = bf16[128,2,512]{2,1,0:T(2,128)(2,1)S(1)} async-done(((bf16[128,2,512]{2,1,0:T(2,128)(2,1)}), bf16[128,2,512]{2,1,0:T(2,128)(2,1)S(1)}, u32[]{:S(2)}, u32[]{:S(2)}) %all-to-all-start) | async-done | bytes 262176 | tf_op jit(solution)/shard_map/all_to_all | solution.py:13
  53.4 0.2 reshape.28
  53.6 93.7 %all-gather.4.cloned.1.call-done = bf16[128,4096]{0,1:T(8,128)(2,1)} async-done(((bf16[128,32]{0,1:T(8,128)(2,1)}), bf16[128,4096]{0,1:T(8,128)(2,1)}) %all-gather.4.cloned.1.call-update) | async-done | bytes 1048592 | tf_op jit(solution)/shard_map/all_gather | solution.py:11
  147.4 87.4 %all-gather.6.cloned.1.call-done = bf16[4096,1024]{1,0:T(8,128)(2,1)} async-done(((bf16[1024,1024]{1,0:T(8,128)(2,1)}), bf16[4096,1024]{1,0:T(8,128)(2,1)}) %all-gather.6.cloned.1.call-update) | async-done | bytes 8388624 | tf_op jit(solution)/shard_map/all_gather | solution.py:14
  234.8 5.1 fusion.1
  239.8 252.8 %pmax.7 = f32[128]{0:T(128)S(1)} all-reduce(f32[128]{0:T(128)S(1)} %get-tuple-element.19), channel_id=1, replica_groups=mesh['dp'=4,'vocab'=128] {'vocab'}, use_global_device_ids=true, to_apply=%region_1.0 | all-reduce | flops 128 | bytes 1024 | tf_op jit(solution)/shard_map/pmax | solution.py:17
  492.7 0.3 fusion
  493.0 246.8 %all-reduce = (f32[128]{0:T(128)S(1)}, f32[128]{0:T(128)S(1)}) all-reduce(f32[128]{0:T(128)S(1)} %get-tuple-element.16, f32[128]{0:T(128)S(1)} %get-tuple-element.15), channel_id=1, replica_groups=mesh['dp'=4,'vocab'=128] {'vocab'}, use_global_device_ids=true, to_apply=%region_5.0 | all-reduce | flops 256 | bytes 2048 | tf_op jit(solution)/shard_map/psum | solution.py:19
  739.8 1.1 multiply_convert_fusion
  740.9 0.0 reduce-scatter.2.cloned.1.call-start
  741.0 7.2 fusion.2
  748.2 26.7 %all_to_all.32 = bf16[128,4,1024]{0,2,1:T(8,128)(2,1)S(1)} all-to-all(bf16[128,4,1024]{0,2,1:T(8,128)(2,1)S(1)} %bitcast.18), channel_id=1, replica_groups=mesh['dp'=4,'vocab'=128] {'dp'}, dimensions={1} | all-to-all | bytes 2097152 | tf_op jit(solution)/shard_map/all_to_all | solution.py:12
  774.9 0.5 copy.13
  775.5 2.5 convert_bitcast_fusion
  778.0 2.6 copy.14
  780.6 257.3 %reduce-scatter.2.cloned.1.call-done = f32[128,32]{0,1:T(8,128)} async-done(((f32[128,4096]{0,1:T(8,128)}), f32[128,32]{0,1:T(8,128)}) %reduce-scatter.2.cloned.1.call-update) | async-done | bytes 16400 | tf_op jit(solution)/shard_map/reduce_scatter | solution.py:36
  (11 shorter events, 0.1 us)
Async XLA Ops:
  7.2 140.2 %all-gather.4.cloned.1.call-start = ((), (), s32[]{:S(2)}) async-start(), calls=%async_computation.3 | async-start | bytes 1056768 | tf_op jit(solution)/shard_map/all_gather | solution.py:11
  7.9 226.9 %all-gather.6.cloned.1.call-start = ((), (), s32[]{:S(2)}) async-start(), calls=%async_computation.4 | async-start | bytes 10485760 | tf_op jit(solution)/shard_map/all_gather | solution.py:14
  13.2 40.2 %all-to-all-start = ((bf16[128,2,512]{2,1,0:T(2,128)(2,1)}), bf16[128,2,512]{2,1,0:T(2,128)(2,1)S(1)}, u32[]{:S(2)}, u32[]{:S(2)}) async-start(bf16[128,2,512]{2,1,0:T(2,128)(2,1)} %reshape.27), calls=%async_computation | async-start | bytes 524288 | tf_op jit(solution)/shard_map/all_to_all | solution.py:13
  33.1 742.4 %all-gather.8.cloned.1.call-start = ((), (), s32[]{:S(2)}) async-start(), calls=%async_computation.6 | async-start | bytes 1310720 | tf_op jit(solution)/shard_map/all_gather | solution.py:29
  53.6 686.2 %copy-start.1 = (s32[128]{0:T(128)S(1)}, s32[128]{0:T(128)}, u32[]{:S(2)}) copy-start(s32[128]{0:T(128)} %param.8) | copy-start | bytes 1540
  239.8 508.4 %copy-start = (bf16[128,4096]{0,1:T(8,128)(2,1)S(1)}, bf16[128,4096]{0,1:T(8,128)(2,1)}, u32[]{:S(2)}) copy-start(bf16[128,4096]{0,1:T(8,128)(2,1)} %all-gather.4.cloned.1.call-done) | copy-start | bytes 3145732
  740.9 297.0 %reduce-scatter.2.cloned.1.call-start = ((), (), s32[]{:S(2)}) async-start(), calls=%async_computation.5 | async-start | bytes 2113536 | tf_op jit(solution)/shard_map/reduce_scatter | solution.py:36
Sparse Core Ops, SparseCore 0:
  11.0 136.3 all-gather.3
  149.5 85.2 all-gather.5
  741.0 34.3 all-gather.7
  780.5 257.3 reduce-scatter.1
where the time goes:
time: 1040 us
  blocking collectives  526 us (51%)
  waiting for transfers between devices  459 us (44%)
  starting transfers between devices  20.1 us (2%)
  matrix products  14.8 us (1%)
  between operations  13.8 us (1%)
    reduce_scatter x1, waiting for transfers between devices, local(): lax.psum_scatter(feature_part, 'vocab', scatter_dimension=1, tiled=True)  257 us
    pmax x1, blocking collectives, local(): top = lax.pmax(jnp.max(logits, axis=1), 'vocab')  253 us
    psum x1, blocking collectives, local(): lax.psum((jnp.sum(expo, axis=1), jnp.sum(expo * gap, axis=1)), 'vocab')  247 us
    all_gather x1, waiting for transfers between devices, local(): hidden_full = lax.all_gather(hidden_states, 'vocab', axis=1, tiled=True)  93.7 us
    all_gather x1, waiting for transfers between devices, local(): head_full = lax.all_gather(head_weight, 'dp', axis=0, tiled=True)  87.4 us
    all_to_all x1, blocking collectives, local(): lax.all_to_all(hidden_full, 'dp', split_axis=1, concat_axis=0, tiled=True)  26.7 us
  transfers between devices with their start and end apart: 5, of which 4 were waited for; matrix products, arithmetic and copies ran while one was open for 2% of the time, Pallas kernels for 0%

commit v1 on v0

v1 whole, which is shorter than its diff:
```python
import jax
import jax.numpy as jnp
from jax import lax
from jax.sharding import Mesh, PartitionSpec as P

anchor_weight = 0.25

X, Z, Y, C = 4, 16, 4, 2
K = Z // X
TOK = 128
FEAT = 32
ROWS = 1024
COLS = 1024

f32 = jnp.float32
bf16 = jnp.bfloat16


def shift(value, axis, size, step):
    return lax.ppermute(value, axis, [(i, (i + step) % size) for i in range(size)])


def spread(value, axes, size):
    sent = jnp.broadcast_to(value[None], (size,) + value.shape)
    return lax.all_to_all(sent, axes, 0, 0, tiled=True)


def merge(parts):
    top = jnp.max(parts[:, 0], axis=0)
    scale = jnp.exp(parts[:, 0] - top[None])
    return jnp.stack(
        [top, jnp.sum(scale * parts[:, 1], axis=0), jnp.sum(scale * parts[:, 2], axis=0)]
    )


def gather_hidden(hidden_states):
    mine = spread(hidden_states.T, "z", Z)
    sent = jnp.broadcast_to(mine.reshape(X, 1, K, FEAT, TOK), (X, Y, K, FEAT, TOK))
    here = lax.all_to_all(sent.reshape(X * Y, K, FEAT, TOK), ("x", "y"), 0, 0, tiled=True)
    there = shift(here, "c", C, 1)
    first = lax.axis_index("c") == 0
    both = jnp.stack([jnp.where(first, here, there), jnp.where(first, there, here)])
    both = both.reshape(C, X, Y, K, FEAT, TOK)
    return both.transpose(1, 3, 2, 0, 4, 5).reshape(X, ROWS, TOK)


def local(hidden_states, teacher_logprob, head_weight, token_ids, padding_mask):
    me = lax.axis_index("x")
    hidden = gather_hidden(hidden_states)
    partial = lax.dot_general(
        hidden, head_weight, (((1,), (0,)), ((), ())), preferred_element_type=f32
    )
    logits = lax.dynamic_index_in_dim(partial, me, 0, keepdims=False)
    for step in (2, 1, 3):
        chunk = lax.dynamic_index_in_dim(partial, lax.rem(me + step, X), 0, keepdims=False)
        logits = logits + shift(chunk, "x", X, step)

    teacher = lax.all_to_all(
        teacher_logprob, ("z", "y", "c"), split_axis=1, concat_axis=0, tiled=True
    )
    gap = logits - teacher.astype(f32)
    top = jnp.max(logits, axis=1)
    expo = jnp.exp(logits - top[:, None])
    stats = jnp.stack([top, jnp.sum(expo, axis=1), jnp.sum(expo * gap, axis=1)])
    stats = merge(spread(stats, ("y", "c"), Y * C))
    stats = merge(spread(stats, "z", Z))
    whole, total, weighted = stats[0], stats[1], stats[2]

    start = (
        (lax.axis_index("z") * Y + lax.axis_index("y")) * C + lax.axis_index("c")
    ) * COLS
    columns = start + jnp.arange(COLS, dtype=jnp.int32)
    onehot = (columns[None, :] == token_ids[:, None]).astype(f32)
    prob = jnp.exp(logits - whole[:, None]) / total[:, None]
    keep = padding_mask.astype(f32)[:, None]
    logit_grad = (
        keep * (prob * (gap - (weighted / total)[:, None]) + anchor_weight * (prob - onehot))
    ).astype(bf16)

    grads = spread(logit_grad, "x", X).reshape(X * TOK, COLS)
    feature = lax.dot_general(
        head_weight, grads, (((1,), (1,)), ((), ())), preferred_element_type=f32
    ).astype(bf16)
    feature = feature.reshape(K, Y, C, FEAT, X, TOK)
    cme = lax.axis_index("c")
    sent = lax.dynamic_index_in_dim(feature, 1 - cme, 2, keepdims=False)
    kept = lax.dynamic_index_in_dim(feature, cme, 2, keepdims=False)
    pair = kept.astype(f32) + shift(sent, "c", C, 1).astype(f32)
    pair = pair.astype(bf16).transpose(3, 1, 0, 2, 4).reshape(X * Y, K, FEAT, TOK)
    plane = lax.all_to_all(pair, ("x", "y"), 0, 0, tiled=True)
    plane = jnp.sum(plane.reshape(X, Y, K, FEAT, TOK).astype(f32), axis=1).astype(bf16)
    line = lax.all_to_all(plane.reshape(Z, FEAT, TOK), "z", 0, 0, tiled=True)
    hidden_grad = jnp.sum(line.astype(f32), axis=0).T

    head_grad = lax.dot_general(
        hidden.transpose(1, 0, 2).reshape(ROWS, X * TOK),
        grads,
        (((1,), (0,)), ((), ())),
        preferred_element_type=f32,
    ).astype(bf16)
    return (logit_grad, hidden_grad, head_grad)


def solution(mesh):
    inner = Mesh(mesh.devices.reshape(X, Z, Y, C), ("x", "z", "y", "c"))
    v = ("z", "y", "c")
    in_specs = (P("x", v), P(("x",) + v, None), P("x", v), P("x"), P("x"))
    out_specs = (P("x", v), P("x", v), P("x", v))
    return jax.shard_map(local, mesh=inner, in_specs=in_specs, out_specs=out_specs, check_vma=False)
```

time: 1040 us -> 197 us (0.19)
  blocking collectives: 526 us -> 59.7 us
  waiting for transfers between devices: 459 us -> 59.9 us
  starting transfers between devices: 20.1 us -> 46.4 us
  between operations: 13.8 us -> 0.96 us
    reduce_scatter x1 -> x0, waiting for transfers between devices: 257 us -> none  [local(): lax.psum_scatter(feature_part, 'vocab', scatter_dimension=1, tiled=True)]
    pmax x1 -> x0, blocking collectives: 253 us -> none  [local(): top = lax.pmax(jnp.max(logits, axis=1), 'vocab')]
    psum x1 -> x0, blocking collectives: 247 us -> none  [local(): lax.psum((jnp.sum(expo, axis=1), jnp.sum(expo * gap, axis=1)), 'vocab')]
    all_gather x3 -> x0, waiting for transfers between devices: 181 us -> none  [the longest x1 93.7 us: local(): hidden_full = lax.all_gather(hidden_states, 'vocab', axis=1, tiled=True)]
    all_to_all x1 -> x3, blocking collectives: 26.7 us -> 59.7 us  [the longest x1 29.7 us: spread(): return lax.all_to_all(sent, axes, 0, 0, tiled=True)]
    all_to_all x1 -> x5, waiting for transfers between devices: 19.5 us -> 46.1 us  [the longest x3 29.8 us: spread(): return lax.all_to_all(sent, axes, 0, 0, tiled=True)]
    ppermute x0 -> x5, waiting for transfers between devices: none -> 13.9 us  [shift(): lax.ppermute(value, axis, [(i, (i + step) % size) for i in range(size)])]
    ppermute x0 -> x5, starting transfers between devices: none -> 13.5 us  [shift(): lax.ppermute(value, axis, [(i, (i + step) % size) for i in range(size)])]
  transfers between devices with their start and end apart: 5 -> 10, of which waited for: 4 -> 9; matrix products, arithmetic and copies ran while one was open for 2% -> 6% of each run, Pallas kernels for 0% -> 0%
where the time goes in v1:
time: 197 us; the launch traced here: 196 us
  waiting for transfers between devices  59.9 us (30%)
  blocking collectives  59.7 us (30%)
  starting transfers between devices  46.4 us (24%)
  local copies, waits for them, and re-layouts  12.5 us (6%)
  other arithmetic  9.13 us (5%)
  matrix products  7.32 us (4%)
    all_to_all x3, waiting for transfers between devices, spread(): return lax.all_to_all(sent, axes, 0, 0, tiled=True)  29.8 us
    all_to_all x1, blocking collectives, spread(): return lax.all_to_all(sent, axes, 0, 0, tiled=True)  29.7 us
    all_to_all x3, starting transfers between devices, spread(): return lax.all_to_all(sent, axes, 0, 0, tiled=True)  22 us
    all_to_all x1, blocking collectives, gather_hidden(): lax.all_to_all(sent.reshape(X * Y, K, FEAT, TOK), ('x', 'y'), 0, 0, tiled...  15.3 us
    all_to_all x1, blocking collectives, local(): plane = lax.all_to_all(pair, ('x', 'y'), 0, 0, tiled=True)  14.7 us
    ppermute x5, waiting for transfers between devices, shift(): lax.ppermute(value, axis, [(i, (i + step) % size) for i in range(size)])  13.9 us
    ppermute x5, starting transfers between devices, shift(): lax.ppermute(value, axis, [(i, (i + step) % size) for i in range(size)])  13.5 us
    all_to_all x1, waiting for transfers between devices, local(): line = lax.all_to_all(plane.reshape(Z, FEAT, TOK), 'z', 0, 0, tiled=True)  10 us
  transfers between devices with their start and end apart: 10, of which 9 were waited for; matrix products, arithmetic and copies ran while one was open for 6% of the time, Pallas kernels for 0%

profile of v1, /device:TPU:6, one launch (start us, length us, event | category | flops | bytes accessed | tf_op | source)
XLA Modules:
  0.0 195.9 jit_solution(18288220824496879475)
XLA Ops:
  1.5 29.7 %all_to_all.48 = bf16[16,32,128]{2,1,0:T(8,128)(2,1)S(1)} all-to-all(bf16[16,32,128]{2,1,0:T(8,128)(2,1)S(1)} %broadcast_in_dim.12), channel_id=1, replica_groups=mesh['x'=4,'z'=16,'y'=4,'c'=2] {'z'}, dimensions={0} | all-to-all | bytes 262144 | tf_op jit(solution)/shard_map/all_to_all | solution.py:25
  31.3 15.3 %all_to_all.49 = bf16[16,4,32,128]{3,2,1,0:T(8,128)(2,1)S(1)} all-to-all(bf16[16,4,32,128]{3,2,1,0:T(8,128)(2,1)S(1)} %bitcast.80), channel_id=1, replica_groups=mesh['x'=4,'z'=16,'y'=4,'c'=2] {'x','y'}, dimensions={0} | all-to-all | bytes 1048576 | tf_op jit(solution)/shard_map/all_to_all | solution.py:39
  46.6 1.9 collective-permute-start
  49.0 3.1 %reduce.3 = bf16[128,1024]{1,0:T(8,128)(2,1)S(1)} reduce(bf16[128,1,1024]{2,1,0:T(2,128)(2,1)} %bitcast.86, bf16[]{:T(256)} %broadcast.18), dimensions={1}, to_apply=%bitcast.69.reduce_sub_computation | reduce | bytes 524290
  53.0 7.4 %all-to-all-start.2 = ((bf16[128,2,512]{2,1,0:T(2,128)(2,1)}), bf16[128,2,512]{2,1,0:T(2,128)(2,1)S(1)}, u32[]{:S(2)}, u32[]{:S(2)}) async-start(bf16[128,2,512]{2,1,0:T(2,128)(2,1)} %reshape.76), calls=%async_computation.2 | async-start | bytes 524288 | tf_op jit(solution)/shard_map/all_to_all | solution.py:58
  64.6 3.8 %collective-permute-start.1 = (f32[128,1024]{1,0:T(8,128)}, f32[128,1024]{1,0:T(8,128)}, u32[]{:S(2)}, u32[]{:S(2)}) collective-permute-start(f32[128,1024]{1,0:T(8,128)} %get-tuple-element.11), channel_id=1, source_target_pairs={{0,256},{128,384},{256,0},{384,128},{1,257},{129,385},{257,1},{385... | collective-permute-start | bytes 1572872 | tf_op jit(solution)/shard_map/ppermute | solution.py:20
  68.4 3.7 %collective-permute-start.2 = (f32[128,1024]{1,0:T(8,128)}, f32[128,1024]{1,0:T(8,128)}, u32[]{:S(2)}, u32[]{:S(2)}) collective-permute-start(f32[128,1024]{1,0:T(8,128)} %get-tuple-element.13), channel_id=1, source_target_pairs={{0,128},{128,256},{256,384},{384,0},{1,129},{129,257},{257,385},{3... | collective-permute-start | bytes 1572872 | tf_op jit(solution)/shard_map/ppermute | solution.py:20
  72.1 2.2 %collective-permute-start.3 = (f32[128,1024]{1,0:T(8,128)}, f32[128,1024]{1,0:T(8,128)}, u32[]{:S(2)}, u32[]{:S(2)}) collective-permute-start(f32[128,1024]{1,0:T(8,128)} %get-tuple-element.12), channel_id=1, source_target_pairs={{0,384},{128,0},{256,128},{384,256},{1,385},{129,1},{257,129},{385... | collective-permute-start | bytes 1572872 | tf_op jit(solution)/shard_map/ppermute | solution.py:20
  74.3 6.2 %all-to-all-done.2 = bf16[128,2,512]{2,1,0:T(2,128)(2,1)S(1)} async-done(((bf16[128,2,512]{2,1,0:T(2,128)(2,1)}), bf16[128,2,512]{2,1,0:T(2,128)(2,1)S(1)}, u32[]{:S(2)}, u32[]{:S(2)}) %all-to-all-start.2) | async-done | bytes 262176 | tf_op jit(solution)/shard_map/all_to_all | solution.py:58
  83.2 9.3 %collective-permute-done.2 = f32[128,1024]{1,0:T(8,128)} collective-permute-done((f32[128,1024]{1,0:T(8,128)}, f32[128,1024]{1,0:T(8,128)}, u32[]{:S(2)}, u32[]{:S(2)}) %collective-permute-start.2) | collective-permute-done | bytes 524320 | tf_op jit(solution)/shard_map/ppermute | solution.py:20
  95.6 4.4 %all-to-all-start.3 = ((f32[8,3,128]{2,1,0:T(4,128)}), f32[8,3,128]{2,1,0:T(4,128)S(1)}, u32[]{:S(2)}, u32[]{:S(2)}) async-start(f32[8,3,128]{2,1,0:T(4,128)} %broadcast_in_dim.15), calls=%async_computation.3 | async-start | bytes 32768 | tf_op jit(solution)/shard_map/all_to_all | solution.py:25
  100.1 5.3 %all-to-all-done.3 = f32[8,3,128]{2,1,0:T(4,128)S(1)} async-done(((f32[8,3,128]{2,1,0:T(4,128)}), f32[8,3,128]{2,1,0:T(4,128)S(1)}, u32[]{:S(2)}, u32[]{:S(2)}) %all-to-all-start.3) | async-done | bytes 12320 | tf_op jit(solution)/shard_map/all_to_all | solution.py:25
  106.1 11.9 %all-to-all-start.4 = ((f32[16,3,128]{2,1,0:T(4,128)}), f32[16,3,128]{2,1,0:T(4,128)S(1)}, u32[]{:S(2)}, u32[]{:S(2)}) async-start(f32[16,3,128]{2,1,0:T(4,128)} %broadcast_in_dim.16), calls=%async_computation.4 | async-start | bytes 65536 | tf_op jit(solution)/shard_map/all_to_all | solution.py:25
  118.0 12.5 %all-to-all-done.4 = f32[16,3,128]{2,1,0:T(4,128)S(1)} async-done(((f32[16,3,128]{2,1,0:T(4,128)}), f32[16,3,128]{2,1,0:T(4,128)S(1)}, u32[]{:S(2)}, u32[]{:S(2)}) %all-to-all-start.4) | async-done | bytes 24608 | tf_op jit(solution)/shard_map/all_to_all | solution.py:25
  132.1 5.7 %all-to-all-start.5 = ((bf16[4,128,1024]{2,1,0:T(8,128)(2,1)}), bf16[4,128,1024]{2,1,0:T(8,128)(2,1)S(1)}, u32[]{:S(2)}, u32[]{:S(2)}) async-start(bf16[4,128,1024]{2,1,0:T(8,128)(2,1)} %broadcast_in_dim.17), calls=%async_computation.5 | async-start | bytes 2097152 | tf_op jit(solution)/shard_map/all_to_all | solution.py:25
  137.8 11.9 %all-to-all-done.5 = bf16[4,128,1024]{2,1,0:T(8,128)(2,1)S(1)} async-done(((bf16[4,128,1024]{2,1,0:T(8,128)(2,1)}), bf16[4,128,1024]{2,1,0:T(8,128)(2,1)S(1)}, u32[]{:S(2)}, u32[]{:S(2)}) %all-to-all-start.5) | async-done | bytes 1048608 | tf_op jit(solution)/shard_map/all_to_all | solution.py:25
  149.7 2.3 %fusion.2 = bf16[1024,512]{0,1:T(8,128)(2,1)} fusion(bf16[512,1024]{1,0:T(8,128)(2,1)S(1)} %bitcast.84, bf16[1024,1024]{1,0:T(8,128)(2,1)S(1)} %copy-done), kind=kOutput, calls=%fused_computation.4 | convolution fusion | flops 1074266112 | bytes 4194304 | tf_op jit(solution)/shard_map/dot_general | solution.py:81
  152.0 2.3 %copy.45 = bf16[1024,512]{1,0:T(8,128)(2,1)} copy(bf16[1024,512]{0,1:T(8,128)(2,1)} %fusion.2) | data formatting | bytes 2097152 | tf_op jit(solution)/shard_map/convert_element_type | solution.py:83
  156.7 1.9 collective-permute-start.4
  158.7 2.2 %collective-permute-done.4 = bf16[4,4,32,4,128]{4,3,2,1,0:T(4,128)(2,1)} collective-permute-done((bf16[4,4,32,4,128]{4,3,2,1,0:T(4,128)(2,1)}, bf16[4,4,32,4,128]{4,3,2,1,0:T(4,128)(2,1)}, u32[]{:S(2)}, u32[]{:S(2)}) %collective-permute-start.4) | collective-permute-done | bytes 524320 | tf_op jit(solution)/shard_map/ppermute | solution.py:20
  162.5 14.7 %all_to_all.50 = bf16[16,4,32,128]{3,2,1,0:T(8,128)(2,1)S(1)} all-to-all(bf16[16,4,32,128]{3,2,1,0:T(8,128)(2,1)S(1)} %bitcast.83), channel_id=1, replica_groups=mesh['x'=4,'z'=16,'y'=4,'c'=2] {'x','y'}, dimensions={0} | all-to-all | bytes 1048576 | tf_op jit(solution)/shard_map/all_to_all | solution.py:90
  177.9 3.5 %all-to-all-start.7 = ((bf16[16,32,128]{2,1,0:T(8,128)(2,1)}), bf16[16,32,128]{2,1,0:T(8,128)(2,1)S(1)}, u32[]{:S(2)}, u32[]{:S(2)}) async-start(bf16[16,32,128]{2,1,0:T(8,128)(2,1)} %bitcast.32), calls=%async_computation.7 | async-start | bytes 262144 | tf_op jit(solution)/shard_map/all_to_all | solution.py:92
  181.4 3.8 %bitcast_convert_fusion = bf16[1024,1024]{1,0:T(8,128)(2,1)} fusion(bf16[1024,4,128]{2,0,1:T(8,128)(2,1)S(1)} %bitcast.79, bf16[4,128,1024]{2,1,0:T(8,128)(2,1)} %copy-done.6), kind=kOutput, calls=%fused_computation | convolution fusion | flops 1074790400 | bytes 4194304 | tf_op jit(solution)/shard_map/dot_general | solution.py:95
  185.2 10.0 %all-to-all-done.7 = bf16[16,32,128]{2,1,0:T(8,128)(2,1)S(1)} async-done(((bf16[16,32,128]{2,1,0:T(8,128)(2,1)}), bf16[16,32,128]{2,1,0:T(8,128)(2,1)S(1)}, u32[]{:S(2)}, u32[]{:S(2)}) %all-to-all-start.7) | async-done | bytes 131104 | tf_op jit(solution)/shard_map/all_to_all | solution.py:92
  (55 shorter events, 19.8 us)
Async XLA Ops:
  0.6 60.2 %copy-start = (bf16[1024,1024]{1,0:T(8,128)(2,1)S(1)}, bf16[1024,1024]{1,0:T(8,128)(2,1)}, u32[]{:S(2)}) copy-start(bf16[1024,1024]{1,0:T(8,128)(2,1)} %param.7) | copy-start | bytes 6291460
  46.6 13.8 %collective-permute-start = (bf16[16,4,32,128]{3,2,1,0:T(8,128)(2,1)S(1)}, bf16[16,4,32,128]{3,2,1,0:T(8,128)(2,1)S(1)}, u32[]{:S(2)}, u32[]{:S(2)}) collective-permute-start(bf16[16,4,32,128]{3,2,1,0:T(8,128)(2,1)S(1)} %all_to_all.49), channel_id=1, source_target_pairs={{0,1},{1,0},{2,3},{3,2},{4,5},{5,4},{6,7},{7,6},{8,9},{9,8},{10,11... | collective-permute-start | bytes 1572872 | tf_op jit(solution)/shard_map/ppermute | solution.py:20
  53.0 27.5 %all-to-all-start.2 = ((bf16[128,2,512]{2,1,0:T(2,128)(2,1)}), bf16[128,2,512]{2,1,0:T(2,128)(2,1)S(1)}, u32[]{:S(2)}, u32[]{:S(2)}) async-start(bf16[128,2,512]{2,1,0:T(2,128)(2,1)} %reshape.76), calls=%async_computation.2 | async-start | bytes 524288 | tf_op jit(solution)/shard_map/all_to_all | solution.py:58
  60.8 1.3 copy-start.2
  62.1 1.3 copy-start.1
  64.6 18.6 %collective-permute-start.1 = (f32[128,1024]{1,0:T(8,128)}, f32[128,1024]{1,0:T(8,128)}, u32[]{:S(2)}, u32[]{:S(2)}) collective-permute-start(f32[128,1024]{1,0:T(8,128)} %get-tuple-element.11), channel_id=1, source_target_pairs={{0,256},{128,384},{256,0},{384,128},{1,257},{129,385},{257,1},{385... | collective-permute-start | bytes 1572872 | tf_op jit(solution)/shard_map/ppermute | solution.py:20
  68.4 24.1 %collective-permute-start.2 = (f32[128,1024]{1,0:T(8,128)}, f32[128,1024]{1,0:T(8,128)}, u32[]{:S(2)}, u32[]{:S(2)}) collective-permute-start(f32[128,1024]{1,0:T(8,128)} %get-tuple-element.13), channel_id=1, source_target_pairs={{0,128},{128,256},{256,384},{384,0},{1,129},{129,257},{257,385},{3... | collective-permute-start | bytes 1572872 | tf_op jit(solution)/shard_map/ppermute | solution.py:20
  72.1 20.9 %collective-permute-start.3 = (f32[128,1024]{1,0:T(8,128)}, f32[128,1024]{1,0:T(8,128)}, u32[]{:S(2)}, u32[]{:S(2)}) collective-permute-start(f32[128,1024]{1,0:T(8,128)} %get-tuple-element.12), channel_id=1, source_target_pairs={{0,384},{128,0},{256,128},{384,256},{1,385},{129,1},{257,129},{385... | collective-permute-start | bytes 1572872 | tf_op jit(solution)/shard_map/ppermute | solution.py:20
  81.3 18.7 %copy-start.8 = (s32[128]{0:T(128)S(1)}, s32[128]{0:T(128)}, u32[]{:S(2)}) copy-start(s32[128]{0:T(128)} %param.9) | copy-start | bytes 1540
  81.3 49.3 %copy-start.7 = (s32[128]{0:T(128)S(1)}, s32[128]{0:T(128)}, u32[]{:S(2)}) copy-start(s32[128]{0:T(128)} %param.8) | copy-start | bytes 1540
  95.6 9.8 %all-to-all-start.3 = ((f32[8,3,128]{2,1,0:T(4,128)}), f32[8,3,128]{2,1,0:T(4,128)S(1)}, u32[]{:S(2)}, u32[]{:S(2)}) async-start(f32[8,3,128]{2,1,0:T(4,128)} %broadcast_in_dim.15), calls=%async_computation.3 | async-start | bytes 32768 | tf_op jit(solution)/shard_map/all_to_all | solution.py:25
  106.1 24.5 %all-to-all-start.4 = ((f32[16,3,128]{2,1,0:T(4,128)}), f32[16,3,128]{2,1,0:T(4,128)S(1)}, u32[]{:S(2)}, u32[]{:S(2)}) async-start(f32[16,3,128]{2,1,0:T(4,128)} %broadcast_in_dim.16), calls=%async_computation.4 | async-start | bytes 65536 | tf_op jit(solution)/shard_map/all_to_all | solution.py:25
  131.0 20.9 %copy-start.5 = (bf16[128,1024]{1,0:T(8,128)(2,1)}, bf16[128,1024]{1,0:T(8,128)(2,1)S(1)}, u32[]{:S(2)}) copy-start(bf16[128,1024]{1,0:T(8,128)(2,1)S(1)} %multiply_convert_fusion) | copy-start | bytes 786436
  132.1 17.6 %all-to-all-start.5 = ((bf16[4,128,1024]{2,1,0:T(8,128)(2,1)}), bf16[4,128,1024]{2,1,0:T(8,128)(2,1)S(1)}, u32[]{:S(2)}, u32[]{:S(2)}) async-start(bf16[4,128,1024]{2,1,0:T(8,128)(2,1)} %broadcast_in_dim.17), calls=%async_computation.5 | async-start | bytes 2097152 | tf_op jit(solution)/shard_map/all_to_all | solution.py:25
  149.7 2.3 %copy-start.6 = (bf16[4,128,1024]{2,1,0:T(8,128)(2,1)}, bf16[4,128,1024]{2,1,0:T(8,128)(2,1)S(1)}, u32[]{:S(2)}) copy-start(bf16[4,128,1024]{2,1,0:T(8,128)(2,1)S(1)} %all-to-all-done.5) | copy-start | bytes 3145732
  155.6 3.1 %copy-start.4 = (bf16[4,4,2,32,4,128]{5,4,3,2,1,0:T(4,128)(2,1)}, bf16[4,4,2,32,4,128]{5,4,3,2,1,0:T(4,128)(2,1)S(1)}, u32[]{:S(2)}) copy-start(bf16[4,4,2,32,4,128]{5,4,3,2,1,0:T(4,128)(2,1)S(1)} %reshape.68) | copy-start | bytes 3145732
  156.7 4.1 %collective-permute-start.4 = (bf16[4,4,32,4,128]{4,3,2,1,0:T(4,128)(2,1)}, bf16[4,4,32,4,128]{4,3,2,1,0:T(4,128)(2,1)}, u32[]{:S(2)}, u32[]{:S(2)}) collective-permute-start(bf16[4,4,32,4,128]{4,3,2,1,0:T(4,128)(2,1)} %dynamic-slice_bitcast_fusion), channel_id=1, source_target_pairs={{0,1},{1,0},{2,3},{3,2},{4,5},{5,4},{6,7},{7,6},{8,9},{9,8},{10,11... | collective-permute-start | bytes 1572872 | tf_op jit(solution)/shard_map/ppermute | solution.py:20
  158.7 22.7 %copy-start.3 = (bf16[4,4,4,2,32,128]{5,4,3,2,1,0:T(8,128)(2,1)S(1)}, bf16[4,4,4,2,32,128]{5,4,3,2,1,0:T(8,128)(2,1)}, u32[]{:S(2)}) copy-start(bf16[4,4,4,2,32,128]{5,4,3,2,1,0:T(8,128)(2,1)} %copy-done.2) | copy-start | bytes 3145732
  177.9 17.4 %all-to-all-start.7 = ((bf16[16,32,128]{2,1,0:T(8,128)(2,1)}), bf16[16,32,128]{2,1,0:T(8,128)(2,1)S(1)}, u32[]{:S(2)}, u32[]{:S(2)}) async-start(bf16[16,32,128]{2,1,0:T(8,128)(2,1)} %bitcast.32), calls=%async_computation.7 | async-start | bytes 262144 | tf_op jit(solution)/shard_map/all_to_all | solution.py:92

commit v2 on v1

v2 whole, which is shorter than its diff:
```python
import jax
import jax.numpy as jnp
from jax import lax
from jax.experimental import pallas as pl
from jax.experimental.pallas import tpu as pltpu
from jax.sharding import Mesh, PartitionSpec as P

anchor_weight = 0.25

X, Z, Y, C = 4, 16, 4, 2
K = Z // X
TOK = 128
FEAT = 32
ROWS = 1024
COLS = 1024
ADD_COST = 6 * 10**9
LIMIT = 48 * 1024 * 1024

f32 = jnp.float32
bf16 = jnp.bfloat16
STEPS = (2, 1, 3, 0)


def shift(value, axis, size, step):
    return lax.ppermute(value, axis, [(i, (i + step) % size) for i in range(size)])


def spread(value, axes, size):
    sent = jnp.broadcast_to(value[None], (size,) + value.shape)
    return lax.all_to_all(sent, axes, 0, 0, tiled=True)


def merge(parts):
    top = jnp.max(parts[:, 0], axis=0)
    scale = jnp.exp(parts[:, 0] - top[None])
    return jnp.stack(
        [top, jnp.sum(scale * parts[:, 1], axis=0), jnp.sum(scale * parts[:, 2], axis=0)]
    )


def gather_hidden(hidden_states):
    mine = spread(hidden_states.T, "z", Z)
    sent = jnp.broadcast_to(mine.reshape(X, 1, K, FEAT, TOK), (X, Y, K, FEAT, TOK))
    here = lax.all_to_all(sent.reshape(X * Y, K, FEAT, TOK), ("x", "y"), 0, 0, tiled=True)
    return here, shift(here, "c", C, 1)


def partial_kernel(place, here, there, head, far, up, down, own, hidden_t, lhs):
    me, core = place[0], place[1]
    outs = (far, up, down, own)
    for t in range(X):
        for k in range(K):
            for y in range(Y):
                row = (k * Y + y) * C * FEAT
                for mine, ref in ((core, here), (1 - core, there)):
                    at = pl.ds(pl.multiple_of(row + mine * FEAT, FEAT), FEAT)
                    piece = ref[t * Y + y, k]
                    lhs[t, at, :] = piece
                    hidden_t[at, t * TOK : (t + 1) * TOK] = piece
    for step, out in zip(STEPS, outs):
        t = lax.rem(me + step, X)
        out[...] = lax.dot_general(
            lhs[t], head[...], (((0,), (0,)), ((), ())), preferred_element_type=f32
        )


def partial_logits(place, here, there, head):
    vmem = pl.BlockSpec(memory_space=pltpu.VMEM)
    chunk = jax.ShapeDtypeStruct((TOK, COLS), f32)
    return pl.pallas_call(
        partial_kernel,
        out_shape=(chunk,) * X + (jax.ShapeDtypeStruct((ROWS, X * TOK), bf16),),
        in_specs=[pl.BlockSpec(memory_space=pltpu.SMEM), vmem, vmem, vmem],
        out_specs=(vmem,) * (X + 1),
        scratch_shapes=[pltpu.VMEM((X, ROWS, TOK), bf16)],
        compiler_params=pltpu.CompilerParams(vmem_limit_bytes=LIMIT),
        cost_estimate=pl.CostEstimate(
            flops=2 * X * TOK * ROWS * COLS, bytes_accessed=6 << 20, transcendentals=0
        ),
        name="partial_logits",
    )(place, here, there, head)


def add_kernel(own, far, total):
    total[...] = own[...] + far[...]


def add_far(own, far):
    rows = pl.BlockSpec((TOK // 2, COLS), lambda i: (i, 0))
    return pl.pallas_call(
        add_kernel,
        out_shape=jax.ShapeDtypeStruct((TOK, COLS), f32),
        grid=(2,),
        in_specs=[rows, rows],
        out_specs=rows,
        compiler_params=pltpu.CompilerParams(vmem_limit_bytes=LIMIT),
        cost_estimate=pl.CostEstimate(flops=ADD_COST, bytes_accessed=3 << 19, transcendentals=0),
        name="add_far",
    )(own, far)


def feature_kernel(place, grads, head, sent, kept):
    first = place[1] == 0
    band = Y * C * FEAT
    for k in range(K):
        part = lax.dot_general(
            head[k * band : (k + 1) * band, :],
            grads[...],
            (((1,), (1,)), ((), ())),
            preferred_element_type=f32,
        )
        for y in range(Y):
            low = part[y * C * FEAT : y * C * FEAT + FEAT]
            high = part[y * C * FEAT + FEAT : (y + 1) * C * FEAT]
            keep = jnp.where(first, low, high)
            give = jnp.where(first, high, low).astype(bf16)
            for t in range(X):
                kept[t * Y + y, k] = keep[:, t * TOK : (t + 1) * TOK]
                sent[t * Y + y, k] = give[:, t * TOK : (t + 1) * TOK]


def feature_parts(place, grads, head):
    vmem = pl.BlockSpec(memory_space=pltpu.VMEM)
    shape = (X * Y, K, FEAT, TOK)
    return pl.pallas_call(
        feature_kernel,
        out_shape=(jax.ShapeDtypeStruct(shape, bf16), jax.ShapeDtypeStruct(shape, f32)),
        in_specs=[pl.BlockSpec(memory_space=pltpu.SMEM), vmem, vmem],
        out_specs=(vmem, vmem),
        compiler_params=pltpu.CompilerParams(vmem_limit_bytes=LIMIT),
        cost_estimate=pl.CostEstimate(
            flops=2 * X * TOK * ROWS * COLS, bytes_accessed=5 << 20, transcendentals=0
        ),
        name="feature_parts",
    )(place, grads, head)


def local(hidden_states, teacher_logprob, head_weight, token_ids, padding_mask):
    place = jnp.stack([lax.axis_index("x"), lax.axis_index("c")]).astype(jnp.int32)
    here, there = gather_hidden(hidden_states)
    teacher = teacher_logprob.reshape(Z * Y * C, 2, COLS // 2)
    teacher, there = lax.optimization_barrier((teacher, there))
    far, up, down, own, hidden_t = partial_logits(place, here, there, head_weight)
    teacher, own = lax.optimization_barrier((teacher, own))
    teacher = lax.all_to_all(teacher, ("z", "y", "c"), 0, 0, tiled=True).reshape(TOK, COLS)
    logits = add_far(own, shift(far, "x", X, 2)) + (shift(up, "x", X, 1) + shift(down, "x", X, 3))
    gap = logits - teacher.astype(f32)
    top = jnp.max(logits, axis=1)
    expo = jnp.exp(logits - top[:, None])
    stats = jnp.stack([top, jnp.sum(expo, axis=1), jnp.sum(expo * gap, axis=1)])
    stats = merge(spread(stats, ("y", "c"), Y * C))
    stats = merge(spread(stats, "z", Z))
    whole, total, weighted = stats[0], stats[1], stats[2]

    start = (
        (lax.axis_index("z") * Y + lax.axis_index("y")) * C + lax.axis_index("c")
    ) * COLS
    columns = start + jnp.arange(COLS, dtype=jnp.int32)
    onehot = (columns[None, :] == token_ids[:, None]).astype(f32)
    prob = jnp.exp(logits - whole[:, None]) / total[:, None]
    keep = padding_mask.astype(f32)[:, None]
    logit_grad = (
        keep * (prob * (gap - (weighted / total)[:, None]) + anchor_weight * (prob - onehot))
    ).astype(bf16)

    grads = spread(logit_grad, "x", X).reshape(X * TOK, COLS)
    sent, kept = feature_parts(place, grads, head_weight)
    pair = (kept + shift(sent, "c", C, 1).astype(f32)).astype(bf16)
    plane = lax.all_to_all(pair, ("x", "y"), 0, 0, tiled=True)
    plane = jnp.sum(plane.reshape(X, Y, K, FEAT, TOK).astype(f32), axis=1).astype(bf16)
    line = lax.all_to_all(plane.reshape(Z, FEAT, TOK), "z", 0, 0, tiled=True)
    hidden_grad = jnp.sum(line.astype(f32), axis=0).T

    head_grad = jnp.dot(hidden_t, grads, preferred_element_type=f32).astype(bf16)
    return (logit_grad, hidden_grad, head_grad)


def solution(mesh):
    inner = Mesh(mesh.devices.reshape(X, Z, Y, C), ("x", "z", "y", "c"))
    v = ("z", "y", "c")
    in_specs = (P("x", v), P(("x",) + v, None), P("x", v), P("x"), P("x"))
    out_specs = (P("x", v), P("x", v), P("x", v))
    return jax.shard_map(local, mesh=inner, in_specs=in_specs, out_specs=out_specs, check_vma=False)
```

time: 197 us -> 180 us (0.914)
  blocking collectives: 59.7 us -> 75.7 us
  waiting for transfers between devices: 59.9 us -> 45 us
  local copies, waits for them, and re-layouts: 12.5 us -> 4.11 us
  starting transfers between devices: 46.4 us -> 40.7 us
  other arithmetic: 9.13 us -> 3.99 us
  Pallas kernels: 0 us -> 5.14 us
  matrix products: 7.32 us -> 2.57 us
    all_to_all x1 -> x2, blocking collectives: 29.7 us -> 45.8 us  [spread(): return lax.all_to_all(sent, axes, 0, 0, tiled=True)]
    all_to_all x3 -> x2, waiting for transfers between devices: 29.8 us -> 17.9 us  [spread(): return lax.all_to_all(sent, axes, 0, 0, tiled=True)]
    all_to_all x1, waiting for transfers between devices: 6.22 us -> 0.01 us  [local(): lax.all_to_all(teacher, ('z', 'y', 'c'), 0, 0, tiled=True)]
    all_to_all x3 -> x2, starting transfers between devices: 22 us -> 16.3 us  [spread(): return lax.all_to_all(sent, axes, 0, 0, tiled=True)]
    pallas_call x0 -> x3, Pallas kernels: none -> 5.14 us  [the longest x1 3.18 us: partial_logits(): pl.pallas_call(partial_kernel, out_shape=(chunk,) * X + (jax.ShapeDtypeSt...]
    dot_general x3 -> x1, matrix products: 7.32 us -> 2.57 us  [local(): jnp.dot(hidden_t, grads, preferred_element_type=f32).astype(bf16)]
    squeeze x2 -> x0, local copies, waits for them, and re-layouts: 2.35 us -> none  [the longest x1 1.22 us: local(): lax.dynamic_index_in_dim(partial, lax.rem(me + step, X), 0, keepdims=False)]
    convert_element_type x1 -> x0, local copies, waits for them, and re-layouts: 2.29 us -> none  [local(): feature = lax.dot_general(head_weight, grads, (((1,), (1,)), ((), ())), p...]
  transfers between devices with their start and end apart: 10 -> 9, of which waited for: 9 -> 7; matrix products, arithmetic and copies ran while one was open for 6% -> 3% of each run, Pallas kernels for 0% -> 0%
where the time goes in v2:
time: 180 us; the launch traced here: 178 us
  blocking collectives  75.7 us (42%)
  waiting for transfers between devices  45 us (25%)
  starting transfers between devices  40.7 us (23%)
  Pallas kernels  5.14 us (3%)
  local copies, waits for them, and re-layouts  4.11 us (2%)
  other arithmetic  3.99 us (2%)
  matrix products  2.57 us (1%)
    all_to_all x2, blocking collectives, spread(): return lax.all_to_all(sent, axes, 0, 0, tiled=True)  45.8 us
    all_to_all x2, waiting for transfers between devices, spread(): return lax.all_to_all(sent, axes, 0, 0, tiled=True)  17.9 us
    all_to_all x2, starting transfers between devices, spread(): return lax.all_to_all(sent, axes, 0, 0, tiled=True)  16.3 us
    ppermute x5, waiting for transfers between devices, shift(): lax.ppermute(value, axis, [(i, (i + step) % size) for i in range(size)])  15.9 us
    all_to_all x1, blocking collectives, gather_hidden(): lax.all_to_all(sent.reshape(X * Y, K, FEAT, TOK), ('x', 'y'), 0, 0, tiled...  15.3 us
    all_to_all x1, blocking collectives, local(): plane = lax.all_to_all(pair, ('x', 'y'), 0, 0, tiled=True)  14.7 us
    ppermute x5, starting transfers between devices, shift(): lax.ppermute(value, axis, [(i, (i + step) % size) for i in range(size)])  13 us
    all_to_all x1, waiting for transfers between devices, local(): line = lax.all_to_all(plane.reshape(Z, FEAT, TOK), 'z', 0, 0, tiled=True)  11.3 us
  transfers between devices with their start and end apart: 9, of which 7 were waited for; matrix products, arithmetic and copies ran while one was open for 3% of the time, Pallas kernels for 0%

profile of v2, /device:TPU:6, one launch (start us, length us, event | category | flops | bytes accessed | tf_op | source)
XLA Modules:
  0.0 178.2 jit_solution(16680339280208427599)
XLA Ops:
  1.4 29.7 %all_to_all.40 = bf16[16,32,128]{2,1,0:T(8,128)(2,1)S(1)} all-to-all(bf16[16,32,128]{2,1,0:T(8,128)(2,1)S(1)} %broadcast_in_dim.12), channel_id=1, replica_groups=mesh['x'=4,'z'=16,'y'=4,'c'=2] {'z'}, dimensions={0} | all-to-all | bytes 262144 | tf_op jit(solution)/shard_map/all_to_all | solution.py:30
  31.2 15.3 %all_to_all.41.here = bf16[16,4,32,128]{3,2,1,0:T(8,128)(2,1)S(1)} all-to-all(bf16[16,4,32,128]{3,2,1,0:T(8,128)(2,1)S(1)} %bitcast.38), channel_id=1, replica_groups=mesh['x'=4,'z'=16,'y'=4,'c'=2] {'x','y'}, dimensions={0} | all-to-all | bytes 1048576 | tf_op jit(solution)/shard_map/all_to_all | solution.py:44
  46.5 1.9 %collective-permute-start = (bf16[16,4,32,128]{3,2,1,0:T(8,128)(2,1)S(1)}, bf16[16,4,32,128]{3,2,1,0:T(8,128)(2,1)S(1)}, u32[]{:S(2)}, u32[]{:S(2)}) collective-permute-start(bf16[16,4,32,128]{3,2,1,0:T(8,128)(2,1)S(1)} %all_to_all.41.here), channel_id=1, source_target_pairs={{0,1},{1,0},{2,3},{3,2},{4,5},{5,4},{6,7},{7,6},{8,9},{9,8},{10,11... | collective-permute-start | bytes 1572872 | tf_op jit(solution)/shard_map/ppermute | solution.py:25
  48.4 1.6 reduce.3
  50.9 3.2 %partial_logits.1 = (f32[128,1024]{1,0:T(8,128)S(1)}, f32[128,1024]{1,0:T(8,128)S(1)}, f32[128,1024]{1,0:T(8,128)S(1)}, f32[128,1024]{1,0:T(8,128)S(1)}, bf16[1024,512]{1,0:T(8,128)(2,1)S(1)}) custom-call(s32[2]{0:T(128)S(1)} %pad_add_fusion.place, bf16[16,4,32,128]{3,2,1,0:T(8,128)(2,1)S(1)} %all_to_all.41.here, ...), custom_call_target="tpu_custom_call" | custom-call | flops 1073741824 | bytes 6291456 | tf_op jit(solution)/shard_map/partial_logits/pallas_call | solution.py:70
  54.1 1.0 copy-done.1
  55.0 3.2 %collective-permute-start.1 = (f32[128,1024]{1,0:T(8,128)S(1)}, f32[128,1024]{1,0:T(8,128)S(1)}, u32[]{:S(2)}, u32[]{:S(2)}) collective-permute-start(f32[128,1024]{1,0:T(8,128)S(1)} %get-tuple-element.18), channel_id=1, source_target_pairs={{0,256},{128,384},{256,0},{384,128},{1,257},{129,385},{257,1},{385... | collective-permute-start | bytes 1572872 | tf_op jit(solution)/shard_map/ppermute | solution.py:25
  58.2 7.9 %all-to-all-start.2 = ((bf16[128,2,512]{2,1,0:T(2,128)(2,1)}), bf16[128,2,512]{2,1,0:T(2,128)(2,1)S(1)}, u32[]{:S(2)}, u32[]{:S(2)}) async-start(bf16[128,2,512]{2,1,0:T(2,128)(2,1)} %reshape.46), calls=%async_computation.2 | async-start | bytes 524288 | tf_op jit(solution)/shard_map/all_to_all | solution.py:145
  66.1 3.7 %collective-permute-start.2 = (f32[128,1024]{1,0:T(8,128)S(1)}, f32[128,1024]{1,0:T(8,128)S(1)}, u32[]{:S(2)}, u32[]{:S(2)}) collective-permute-start(f32[128,1024]{1,0:T(8,128)S(1)} %get-tuple-element.19), channel_id=1, source_target_pairs={{0,128},{128,256},{256,384},{384,0},{1,129},{129,257},{257,385},{3... | collective-permute-start | bytes 1572872 | tf_op jit(solution)/shard_map/ppermute | solution.py:25
  69.8 2.2 %collective-permute-start.3 = (f32[128,1024]{1,0:T(8,128)S(1)}, f32[128,1024]{1,0:T(8,128)S(1)}, u32[]{:S(2)}, u32[]{:S(2)}) collective-permute-start(f32[128,1024]{1,0:T(8,128)S(1)} %get-tuple-element.20), channel_id=1, source_target_pairs={{0,384},{128,0},{256,128},{384,256},{1,385},{129,1},{257,129},{385... | collective-permute-start | bytes 1572872 | tf_op jit(solution)/shard_map/ppermute | solution.py:25
  72.9 10.6 %collective-permute-done.2 = f32[128,1024]{1,0:T(8,128)S(1)} collective-permute-done((f32[128,1024]{1,0:T(8,128)S(1)}, f32[128,1024]{1,0:T(8,128)S(1)}, u32[]{:S(2)}, u32[]{:S(2)}) %collective-permute-start.2) | collective-permute-done | bytes 524320 | tf_op jit(solution)/shard_map/ppermute | solution.py:25
  83.4 2.7 %collective-permute-done.3 = f32[128,1024]{1,0:T(8,128)S(1)} collective-permute-done((f32[128,1024]{1,0:T(8,128)S(1)}, f32[128,1024]{1,0:T(8,128)S(1)}, u32[]{:S(2)}, u32[]{:S(2)}) %collective-permute-start.3) | collective-permute-done | bytes 524320 | tf_op jit(solution)/shard_map/ppermute | solution.py:25
  87.2 5.4 %all-to-all-start.3 = ((f32[8,3,128]{2,1,0:T(4,128)}), f32[8,3,128]{2,1,0:T(4,128)S(1)}, u32[]{:S(2)}, u32[]{:S(2)}) async-start(f32[8,3,128]{2,1,0:T(4,128)} %broadcast_in_dim.15), calls=%async_computation.3 | async-start | bytes 32768 | tf_op jit(solution)/shard_map/all_to_all | solution.py:30
  92.6 5.3 %all-to-all-done.3 = f32[8,3,128]{2,1,0:T(4,128)S(1)} async-done(((f32[8,3,128]{2,1,0:T(4,128)}), f32[8,3,128]{2,1,0:T(4,128)S(1)}, u32[]{:S(2)}, u32[]{:S(2)}) %all-to-all-start.3) | async-done | bytes 12320 | tf_op jit(solution)/shard_map/all_to_all | solution.py:30
  98.7 11.0 %all-to-all-start.4 = ((f32[16,3,128]{2,1,0:T(4,128)}), f32[16,3,128]{2,1,0:T(4,128)S(1)}, u32[]{:S(2)}, u32[]{:S(2)}) async-start(f32[16,3,128]{2,1,0:T(4,128)} %broadcast_in_dim.16), calls=%async_computation.4 | async-start | bytes 65536 | tf_op jit(solution)/shard_map/all_to_all | solution.py:30
  109.6 12.5 %all-to-all-done.4 = f32[16,3,128]{2,1,0:T(4,128)S(1)} async-done(((f32[16,3,128]{2,1,0:T(4,128)}), f32[16,3,128]{2,1,0:T(4,128)S(1)}, u32[]{:S(2)}, u32[]{:S(2)}) %all-to-all-start.4) | async-done | bytes 24608 | tf_op jit(solution)/shard_map/all_to_all | solution.py:30
  122.7 16.1 %all_to_all.42 = bf16[4,128,1024]{2,1,0:T(8,128)(2,1)S(1)} all-to-all(bf16[4,128,1024]{2,1,0:T(8,128)(2,1)S(1)} %broadcast_in_dim.17), channel_id=1, replica_groups=mesh['x'=4,'z'=16,'y'=4,'c'=2] {'x'}, dimensions={0} | all-to-all | bytes 2097152 | tf_op jit(solution)/shard_map/all_to_all | solution.py:30
  138.8 1.9 %feature_parts.1 = (bf16[16,4,32,128]{3,2,1,0:T(8,128)(2,1)S(1)}, f32[16,4,32,128]{3,2,1,0:T(8,128)S(1)}) custom-call(s32[2]{0:T(128)S(1)} %pad_add_fusion.place, bf16[512,1024]{1,0:T(8,128)(2,1)S(1)} %bitcast.35, bf16[1024,1024]{1,0:T(8,128)(2,1)S(1)} %copy-done), custom_call_target="tpu_custom_call" | custom-call | flops 1073741824 | bytes 5242880 | tf_op jit(solution)/shard_map/feature_parts/pallas_call | solution.py:125
  140.7 2.1 %collective-permute-start.4 = (bf16[16,4,32,128]{3,2,1,0:T(8,128)(2,1)S(1)}, bf16[16,4,32,128]{3,2,1,0:T(8,128)(2,1)S(1)}, u32[]{:S(2)}, u32[]{:S(2)}) collective-permute-start(bf16[16,4,32,128]{3,2,1,0:T(8,128)(2,1)S(1)} %get-tuple-element.23), channel_id=1, source_target_pairs={{0,1},{1,0},{2,3},{3,2},{4,5},{5,4},{6,7},{7,6},{8,9},{9,8},{10,11... | collective-permute-start | bytes 1572872 | tf_op jit(solution)/shard_map/ppermute | solution.py:25
  142.8 1.9 %collective-permute-done.4 = bf16[16,4,32,128]{3,2,1,0:T(8,128)(2,1)S(1)} collective-permute-done((bf16[16,4,32,128]{3,2,1,0:T(8,128)(2,1)S(1)}, bf16[16,4,32,128]{3,2,1,0:T(8,128)(2,1)S(1)}, u32[]{:S(2)}, u32[]{:S(2)}) %collective-permute-start.4) | collective-permute-done | bytes 524320 | tf_op jit(solution)/shard_map/ppermute | solution.py:25
  144.8 14.7 %all_to_all.43 = bf16[16,4,32,128]{3,2,1,0:T(8,128)(2,1)S(1)} all-to-all(bf16[16,4,32,128]{3,2,1,0:T(8,128)(2,1)S(1)} %add_convert_fusion), channel_id=1, replica_groups=mesh['x'=4,'z'=16,'y'=4,'c'=2] {'x','y'}, dimensions={0} | all-to-all | bytes 1048576 | tf_op jit(solution)/shard_map/all_to_all | solution.py:169
  160.2 3.5 %all-to-all-start.7 = ((bf16[16,32,128]{2,1,0:T(8,128)(2,1)}), bf16[16,32,128]{2,1,0:T(8,128)(2,1)S(1)}, u32[]{:S(2)}, u32[]{:S(2)}) async-start(bf16[16,32,128]{2,1,0:T(8,128)(2,1)} %bitcast.19), calls=%async_computation.7 | async-start | bytes 262144 | tf_op jit(solution)/shard_map/all_to_all | solution.py:171
  163.7 2.6 %convolution_convert_fusion = bf16[1024,1024]{1,0:T(8,128)(2,1)} fusion(bf16[1024,512]{1,0:T(8,128)(2,1)S(1)} %copy-done.2, bf16[512,1024]{1,0:T(8,128)(2,1)S(1)} %bitcast.36), kind=kOutput, calls=%fused_computation | convolution fusion | flops 1074790400 | bytes 4194304 | tf_op jit(solution)/shard_map/dot_general | solution.py:174
  166.3 11.3 %all-to-all-done.7 = bf16[16,32,128]{2,1,0:T(8,128)(2,1)S(1)} async-done(((bf16[16,32,128]{2,1,0:T(8,128)(2,1)}), bf16[16,32,128]{2,1,0:T(8,128)(2,1)S(1)}, u32[]{:S(2)}, u32[]{:S(2)}) %all-to-all-start.7) | async-done | bytes 131104 | tf_op jit(solution)/shard_map/all_to_all | solution.py:171
  (42 shorter events, 6.4 us)
Async XLA Ops:
  0.6 47.8 %copy-start.4 = (bf16[1,131072]{1,0:T(2,128)(2,1)S(1)}, bf16[1,131072]{1,0:T(2,128)(2,1)}, u32[]{:S(2)}) copy-start(bf16[1,131072]{1,0:T(2,128)(2,1)} %param.6) | copy-start | bytes 786436
  46.5 4.4 %collective-permute-start = (bf16[16,4,32,128]{3,2,1,0:T(8,128)(2,1)S(1)}, bf16[16,4,32,128]{3,2,1,0:T(8,128)(2,1)S(1)}, u32[]{:S(2)}, u32[]{:S(2)}) collective-permute-start(bf16[16,4,32,128]{3,2,1,0:T(8,128)(2,1)S(1)} %all_to_all.41.here), channel_id=1, source_target_pairs={{0,1},{1,0},{2,3},{3,2},{4,5},{5,4},{6,7},{7,6},{8,9},{9,8},{10,11... | collective-permute-start | bytes 1572872 | tf_op jit(solution)/shard_map/ppermute | solution.py:25
  54.1 1.0 copy-start.1
  55.0 17.7 %collective-permute-start.1 = (f32[128,1024]{1,0:T(8,128)S(1)}, f32[128,1024]{1,0:T(8,128)S(1)}, u32[]{:S(2)}, u32[]{:S(2)}) collective-permute-start(f32[128,1024]{1,0:T(8,128)S(1)} %get-tuple-element.18), channel_id=1, source_target_pairs={{0,256},{128,384},{256,0},{384,128},{1,257},{129,385},{257,1},{385... | collective-permute-start | bytes 1572872 | tf_op jit(solution)/shard_map/ppermute | solution.py:25
  58.2 28.0 %all-to-all-start.2 = ((bf16[128,2,512]{2,1,0:T(2,128)(2,1)}), bf16[128,2,512]{2,1,0:T(2,128)(2,1)S(1)}, u32[]{:S(2)}, u32[]{:S(2)}) async-start(bf16[128,2,512]{2,1,0:T(2,128)(2,1)} %reshape.46), calls=%async_computation.2 | async-start | bytes 524288 | tf_op jit(solution)/shard_map/all_to_all | solution.py:145
  66.1 17.3 %collective-permute-start.2 = (f32[128,1024]{1,0:T(8,128)S(1)}, f32[128,1024]{1,0:T(8,128)S(1)}, u32[]{:S(2)}, u32[]{:S(2)}) collective-permute-start(f32[128,1024]{1,0:T(8,128)S(1)} %get-tuple-element.19), channel_id=1, source_target_pairs={{0,128},{128,256},{256,384},{384,0},{1,129},{129,257},{257,385},{3... | collective-permute-start | bytes 1572872 | tf_op jit(solution)/shard_map/ppermute | solution.py:25
  69.8 16.3 %collective-permute-start.3 = (f32[128,1024]{1,0:T(8,128)S(1)}, f32[128,1024]{1,0:T(8,128)S(1)}, u32[]{:S(2)}, u32[]{:S(2)}) collective-permute-start(f32[128,1024]{1,0:T(8,128)S(1)} %get-tuple-element.20), channel_id=1, source_target_pairs={{0,384},{128,0},{256,128},{384,256},{1,385},{129,1},{257,129},{385... | collective-permute-start | bytes 1572872 | tf_op jit(solution)/shard_map/ppermute | solution.py:25
  72.8 19.8 %copy-start.6 = (s32[128]{0:T(128)S(1)}, s32[128]{0:T(128)}, u32[]{:S(2)}) copy-start(s32[128]{0:T(128)} %param.9) | copy-start | bytes 1540
  72.9 49.4 %copy-start.5 = (s32[128]{0:T(128)S(1)}, s32[128]{0:T(128)}, u32[]{:S(2)}) copy-start(s32[128]{0:T(128)} %param.8) | copy-start | bytes 1540
  87.2 10.8 %all-to-all-start.3 = ((f32[8,3,128]{2,1,0:T(4,128)}), f32[8,3,128]{2,1,0:T(4,128)S(1)}, u32[]{:S(2)}, u32[]{:S(2)}) async-start(f32[8,3,128]{2,1,0:T(4,128)} %broadcast_in_dim.15), calls=%async_computation.3 | async-start | bytes 32768 | tf_op jit(solution)/shard_map/all_to_all | solution.py:30
  98.7 23.5 %all-to-all-start.4 = ((f32[16,3,128]{2,1,0:T(4,128)}), f32[16,3,128]{2,1,0:T(4,128)S(1)}, u32[]{:S(2)}, u32[]{:S(2)}) async-start(f32[16,3,128]{2,1,0:T(4,128)} %broadcast_in_dim.16), calls=%async_computation.4 | async-start | bytes 65536 | tf_op jit(solution)/shard_map/all_to_all | solution.py:30
  122.3 16.5 %copy-start = (bf16[1024,1024]{1,0:T(8,128)(2,1)S(1)}, bf16[1024,1024]{1,0:T(8,128)(2,1)}, u32[]{:S(2)}) copy-start(bf16[1024,1024]{1,0:T(8,128)(2,1)} %head.3) | copy-start | bytes 6291460
  122.6 18.1 %copy-start.3 = (bf16[128,1024]{1,0:T(8,128)(2,1)}, bf16[128,1024]{1,0:T(8,128)(2,1)S(1)}, u32[]{:S(2)}) copy-start(bf16[128,1024]{1,0:T(8,128)(2,1)S(1)} %multiply_convert_fusion) | copy-start | bytes 786436
  140.7 23.0 %copy-start.2 = (bf16[1024,512]{1,0:T(8,128)(2,1)S(1)}, bf16[1024,512]{1,0:T(8,128)(2,1)}, u32[]{:S(2)}) copy-start(bf16[1024,512]{1,0:T(8,128)(2,1)} %copy-done.1) | copy-start | bytes 3145732
  140.7 3.9 %collective-permute-start.4 = (bf16[16,4,32,128]{3,2,1,0:T(8,128)(2,1)S(1)}, bf16[16,4,32,128]{3,2,1,0:T(8,128)(2,1)S(1)}, u32[]{:S(2)}, u32[]{:S(2)}) collective-permute-start(bf16[16,4,32,128]{3,2,1,0:T(8,128)(2,1)S(1)} %get-tuple-element.23), channel_id=1, source_target_pairs={{0,1},{1,0},{2,3},{3,2},{4,5},{5,4},{6,7},{7,6},{8,9},{9,8},{10,11... | collective-permute-start | bytes 1572872 | tf_op jit(solution)/shard_map/ppermute | solution.py:25
  160.2 17.4 %all-to-all-start.7 = ((bf16[16,32,128]{2,1,0:T(8,128)(2,1)}), bf16[16,32,128]{2,1,0:T(8,128)(2,1)S(1)}, u32[]{:S(2)}, u32[]{:S(2)}) async-start(bf16[16,32,128]{2,1,0:T(8,128)(2,1)} %bitcast.19), calls=%async_computation.7 | async-start | bytes 262144 | tf_op jit(solution)/shard_map/all_to_all | solution.py:171

commit v3 on v2

--- a/solution.py
+++ b/solution.py
@@ -45,7 +45,7 @@
     return here, shift(here, "c", C, 1)
 
 
-def partial_kernel(place, here, there, head, far, up, down, own, hidden_t, lhs):
+def partial_kernel(place, here, there, head, far, up, down, own, hidden_t, lhs, flat, sem):
     me, core = place[0], place[1]
     outs = (far, up, down, own)
     for t in range(X):
@@ -56,12 +56,15 @@
                     at = pl.ds(pl.multiple_of(row + mine * FEAT, FEAT), FEAT)
                     piece = ref[t * Y + y, k]
                     lhs[t, at, :] = piece
-                    hidden_t[at, t * TOK : (t + 1) * TOK] = piece
+                    flat[at, t * TOK : (t + 1) * TOK] = piece
+    save = pltpu.make_async_copy(flat, hidden_t, sem)
+    save.start()
     for step, out in zip(STEPS, outs):
         t = lax.rem(me + step, X)
         out[...] = lax.dot_general(
             lhs[t], head[...], (((0,), (0,)), ((), ())), preferred_element_type=f32
         )
+    save.wait()
 
 
 def partial_logits(place, here, there, head):
@@ -71,8 +74,12 @@
         partial_kernel,
         out_shape=(chunk,) * X + (jax.ShapeDtypeStruct((ROWS, X * TOK), bf16),),
         in_specs=[pl.BlockSpec(memory_space=pltpu.SMEM), vmem, vmem, vmem],
-        out_specs=(vmem,) * (X + 1),
-        scratch_shapes=[pltpu.VMEM((X, ROWS, TOK), bf16)],
+        out_specs=(vmem,) * X + (pl.BlockSpec(memory_space=pl.ANY),),
+        scratch_shapes=[
+            pltpu.VMEM((X, ROWS, TOK), bf16),
+            pltpu.VMEM((ROWS, X * TOK), bf16),
+            pltpu.SemaphoreType.DMA,
+        ],
         compiler_params=pltpu.CompilerParams(vmem_limit_bytes=LIMIT),
         cost_estimate=pl.CostEstimate(
             flops=2 * X * TOK * ROWS * COLS, bytes_accessed=6 << 20, transcendentals=0
@@ -166,12 +173,13 @@
     grads = spread(logit_grad, "x", X).reshape(X * TOK, COLS)
     sent, kept = feature_parts(place, grads, head_weight)
     pair = (kept + shift(sent, "c", C, 1).astype(f32)).astype(bf16)
+    head_grad = jnp.dot(hidden_t, grads, preferred_element_type=f32).astype(bf16)
+    pair, head_grad = lax.optimization_barrier((pair, head_grad))
     plane = lax.all_to_all(pair, ("x", "y"), 0, 0, tiled=True)
     plane = jnp.sum(plane.reshape(X, Y, K, FEAT, TOK).astype(f32), axis=1).astype(bf16)
     line = lax.all_to_all(plane.reshape(Z, FEAT, TOK), "z", 0, 0, tiled=True)
     hidden_grad = jnp.sum(line.astype(f32), axis=0).T
 
-    head_grad = jnp.dot(hidden_t, grads, preferred_element_type=f32).astype(bf16)
     return (logit_grad, hidden_grad, head_grad)
 
 

time: 180 us -> 179 us (level)
  blocking collectives: 75.7 us -> 92.5 us
  waiting for transfers between devices: 45 us -> 31.9 us
  starting transfers between devices: 40.7 us -> 37.1 us
    all_to_all x0 -> x1, blocking collectives: none -> 16.6 us  [local(): line = lax.all_to_all(plane.reshape(Z, FEAT, TOK), 'z', 0, 0, tiled=True)]
    all_to_all x1 -> x0, waiting for transfers between devices: 11.3 us -> none  [local(): line = lax.all_to_all(plane.reshape(Z, FEAT, TOK), 'z', 0, 0, tiled=True)]
    all_to_all x1 -> x0, starting transfers between devices: 3.51 us -> none  [local(): line = lax.all_to_all(plane.reshape(Z, FEAT, TOK), 'z', 0, 0, tiled=True)]
    ppermute x5, waiting for transfers between devices: 15.9 us -> 14 us  [shift(): lax.ppermute(value, axis, [(i, (i + step) % size) for i in range(size)])]
  transfers between devices with their start and end apart: 9 -> 8, of which waited for: 7 -> 5; matrix products, arithmetic and copies ran while one was open for 3% -> 3% of each run, Pallas kernels for 0% -> 0%
where the time goes in v3:
time: 179 us; the launch traced here: 178 us
  blocking collectives  92.5 us (52%)
  starting transfers between devices  37.1 us (21%)
  waiting for transfers between devices  31.9 us (18%)
  Pallas kernels  5.2 us (3%)
  local copies, waits for them, and re-layouts  4.11 us (2%)
  other arithmetic  3.35 us (2%)
  matrix products  2.57 us (1%)
    all_to_all x2, blocking collectives, spread(): return lax.all_to_all(sent, axes, 0, 0, tiled=True)  45.8 us
    all_to_all x2, waiting for transfers between devices, spread(): return lax.all_to_all(sent, axes, 0, 0, tiled=True)  17.9 us
    all_to_all x1, blocking collectives, local(): line = lax.all_to_all(plane.reshape(Z, FEAT, TOK), 'z', 0, 0, tiled=True)  16.6 us
    all_to_all x2, starting transfers between devices, spread(): return lax.all_to_all(sent, axes, 0, 0, tiled=True)  16.3 us
    all_to_all x1, blocking collectives, gather_hidden(): lax.all_to_all(sent.reshape(X * Y, K, FEAT, TOK), ('x', 'y'), 0, 0, tiled...  15.3 us
    all_to_all x1, blocking collectives, local(): plane = lax.all_to_all(pair, ('x', 'y'), 0, 0, tiled=True)  14.9 us
    ppermute x5, waiting for transfers between devices, shift(): lax.ppermute(value, axis, [(i, (i + step) % size) for i in range(size)])  14 us
    ppermute x5, starting transfers between devices, shift(): lax.ppermute(value, axis, [(i, (i + step) % size) for i in range(size)])  12.8 us
  transfers between devices with their start and end apart: 8, of which 5 were waited for; matrix products, arithmetic and copies ran while one was open for 3% of the time, Pallas kernels for 0%

profile of v3, /device:TPU:6, one launch (start us, length us, event | category | flops | bytes accessed | tf_op | source)
XLA Modules:
  0.0 177.6 jit_solution(8203880600628825923)
XLA Ops:
  0.6 0.8 broadcast_in_dim.12
  1.4 29.7 %all_to_all.40 = bf16[16,32,128]{2,1,0:T(8,128)(2,1)S(1)} all-to-all(bf16[16,32,128]{2,1,0:T(8,128)(2,1)S(1)} %broadcast_in_dim.12), channel_id=1, replica_groups=mesh['x'=4,'z'=16,'y'=4,'c'=2] {'z'}, dimensions={0} | all-to-all | bytes 262144 | tf_op jit(solution)/shard_map/all_to_all | solution.py:30
  31.2 15.3 %all_to_all.41.here = bf16[16,4,32,128]{3,2,1,0:T(8,128)(2,1)S(1)} all-to-all(bf16[16,4,32,128]{3,2,1,0:T(8,128)(2,1)S(1)} %bitcast.38), channel_id=1, replica_groups=mesh['x'=4,'z'=16,'y'=4,'c'=2] {'x','y'}, dimensions={0} | all-to-all | bytes 1048576 | tf_op jit(solution)/shard_map/all_to_all | solution.py:44
  46.5 1.9 %collective-permute-start = (bf16[16,4,32,128]{3,2,1,0:T(8,128)(2,1)S(1)}, bf16[16,4,32,128]{3,2,1,0:T(8,128)(2,1)S(1)}, u32[]{:S(2)}, u32[]{:S(2)}) collective-permute-start(bf16[16,4,32,128]{3,2,1,0:T(8,128)(2,1)S(1)} %all_to_all.41.here), channel_id=1, source_target_pairs={{0,1},{1,0},{2,3},{3,2},{4,5},{5,4},{6,7},{7,6},{8,9},{9,8},{10,11... | collective-permute-start | bytes 1572872 | tf_op jit(solution)/shard_map/ppermute | solution.py:25
  48.4 1.6 reduce.3
  50.0 0.8 reshape.46
  50.9 3.3 %partial_logits.1 = (f32[128,1024]{1,0:T(8,128)S(1)}, f32[128,1024]{1,0:T(8,128)S(1)}, f32[128,1024]{1,0:T(8,128)S(1)}, f32[128,1024]{1,0:T(8,128)S(1)}, bf16[1024,512]{1,0:T(8,128)(2,1)S(1)}) custom-call(s32[2]{0:T(128)S(1)} %pad_add_fusion.place, bf16[16,4,32,128]{3,2,1,0:T(8,128)(2,1)S(1)} %all_to_all.41.here, ...), custom_call_target="tpu_custom_call" | custom-call | flops 1073741824 | bytes 6291456 | tf_op jit(solution)/shard_map/partial_logits/pallas_call | solution.py:73
  54.2 1.0 copy-done.1
  55.2 3.2 %collective-permute-start.1 = (f32[128,1024]{1,0:T(8,128)S(1)}, f32[128,1024]{1,0:T(8,128)S(1)}, u32[]{:S(2)}, u32[]{:S(2)}) collective-permute-start(f32[128,1024]{1,0:T(8,128)S(1)} %get-tuple-element.20), channel_id=1, source_target_pairs={{0,256},{128,384},{256,0},{384,128},{1,257},{129,385},{257,1},{385... | collective-permute-start | bytes 1572872 | tf_op jit(solution)/shard_map/ppermute | solution.py:25
  58.3 7.9 %all-to-all-start.2 = ((bf16[128,2,512]{2,1,0:T(2,128)(2,1)}), bf16[128,2,512]{2,1,0:T(2,128)(2,1)S(1)}, u32[]{:S(2)}, u32[]{:S(2)}) async-start(bf16[128,2,512]{2,1,0:T(2,128)(2,1)} %reshape.46), calls=%async_computation.2 | async-start | bytes 524288 | tf_op jit(solution)/shard_map/all_to_all | solution.py:152
  66.2 3.7 %collective-permute-start.2 = (f32[128,1024]{1,0:T(8,128)S(1)}, f32[128,1024]{1,0:T(8,128)S(1)}, u32[]{:S(2)}, u32[]{:S(2)}) collective-permute-start(f32[128,1024]{1,0:T(8,128)S(1)} %get-tuple-element.21), channel_id=1, source_target_pairs={{0,128},{128,256},{256,384},{384,0},{1,129},{129,257},{257,385},{3... | collective-permute-start | bytes 1572872 | tf_op jit(solution)/shard_map/ppermute | solution.py:25
  69.9 2.2 %collective-permute-start.3 = (f32[128,1024]{1,0:T(8,128)S(1)}, f32[128,1024]{1,0:T(8,128)S(1)}, u32[]{:S(2)}, u32[]{:S(2)}) collective-permute-start(f32[128,1024]{1,0:T(8,128)S(1)} %get-tuple-element.22), channel_id=1, source_target_pairs={{0,384},{128,0},{256,128},{384,256},{1,385},{129,1},{257,129},{385... | collective-permute-start | bytes 1572872 | tf_op jit(solution)/shard_map/ppermute | solution.py:25
  73.0 10.6 %collective-permute-done.2 = f32[128,1024]{1,0:T(8,128)S(1)} collective-permute-done((f32[128,1024]{1,0:T(8,128)S(1)}, f32[128,1024]{1,0:T(8,128)S(1)}, u32[]{:S(2)}, u32[]{:S(2)}) %collective-permute-start.2) | collective-permute-done | bytes 524320 | tf_op jit(solution)/shard_map/ppermute | solution.py:25
  83.6 2.7 %collective-permute-done.3 = f32[128,1024]{1,0:T(8,128)S(1)} collective-permute-done((f32[128,1024]{1,0:T(8,128)S(1)}, f32[128,1024]{1,0:T(8,128)S(1)}, u32[]{:S(2)}, u32[]{:S(2)}) %collective-permute-start.3) | collective-permute-done | bytes 524320 | tf_op jit(solution)/shard_map/ppermute | solution.py:25
  87.3 5.4 %all-to-all-start.3 = ((f32[8,3,128]{2,1,0:T(4,128)}), f32[8,3,128]{2,1,0:T(4,128)S(1)}, u32[]{:S(2)}, u32[]{:S(2)}) async-start(f32[8,3,128]{2,1,0:T(4,128)} %broadcast_in_dim.15), calls=%async_computation.3 | async-start | bytes 32768 | tf_op jit(solution)/shard_map/all_to_all | solution.py:30
  92.7 5.3 %all-to-all-done.3 = f32[8,3,128]{2,1,0:T(4,128)S(1)} async-done(((f32[8,3,128]{2,1,0:T(4,128)}), f32[8,3,128]{2,1,0:T(4,128)S(1)}, u32[]{:S(2)}, u32[]{:S(2)}) %all-to-all-start.3) | async-done | bytes 12320 | tf_op jit(solution)/shard_map/all_to_all | solution.py:30
  98.8 11.0 %all-to-all-start.4 = ((f32[16,3,128]{2,1,0:T(4,128)}), f32[16,3,128]{2,1,0:T(4,128)S(1)}, u32[]{:S(2)}, u32[]{:S(2)}) async-start(f32[16,3,128]{2,1,0:T(4,128)} %broadcast_in_dim.16), calls=%async_computation.4 | async-start | bytes 65536 | tf_op jit(solution)/shard_map/all_to_all | solution.py:30
  109.8 12.5 %all-to-all-done.4 = f32[16,3,128]{2,1,0:T(4,128)S(1)} async-done(((f32[16,3,128]{2,1,0:T(4,128)}), f32[16,3,128]{2,1,0:T(4,128)S(1)}, u32[]{:S(2)}, u32[]{:S(2)}) %all-to-all-start.4) | async-done | bytes 24608 | tf_op jit(solution)/shard_map/all_to_all | solution.py:30
  122.8 16.1 %all_to_all.42 = bf16[4,128,1024]{2,1,0:T(8,128)(2,1)S(1)} all-to-all(bf16[4,128,1024]{2,1,0:T(8,128)(2,1)S(1)} %broadcast_in_dim.17), channel_id=1, replica_groups=mesh['x'=4,'z'=16,'y'=4,'c'=2] {'x'}, dimensions={0} | all-to-all | bytes 2097152 | tf_op jit(solution)/shard_map/all_to_all | solution.py:30
  138.9 1.8 %feature_parts.1 = (bf16[16,4,32,128]{3,2,1,0:T(8,128)(2,1)S(1)}, f32[16,4,32,128]{3,2,1,0:T(8,128)S(1)}) custom-call(s32[2]{0:T(128)S(1)} %pad_add_fusion.place, bf16[512,1024]{1,0:T(8,128)(2,1)S(1)} %bitcast.35, bf16[1024,1024]{1,0:T(8,128)(2,1)S(1)} %copy-done), custom_call_target="tpu_custom_call" | custom-call | flops 1073741824 | bytes 5242880 | tf_op jit(solution)/shard_map/feature_parts/pallas_call | solution.py:132
  140.7 1.9 %collective-permute-start.4 = (bf16[16,4,32,128]{3,2,1,0:T(8,128)(2,1)S(1)}, bf16[16,4,32,128]{3,2,1,0:T(8,128)(2,1)S(1)}, u32[]{:S(2)}, u32[]{:S(2)}) collective-permute-start(bf16[16,4,32,128]{3,2,1,0:T(8,128)(2,1)S(1)} %get-tuple-element.25), channel_id=1, source_target_pairs={{0,1},{1,0},{2,3},{3,2},{4,5},{5,4},{6,7},{7,6},{8,9},{9,8},{10,11... | collective-permute-start | bytes 1572872 | tf_op jit(solution)/shard_map/ppermute | solution.py:25
  142.7 2.6 %convolution_convert_fusion = bf16[1024,1024]{1,0:T(8,128)(2,1)} fusion(bf16[1024,512]{1,0:T(8,128)(2,1)S(1)} %copy-done.2, bf16[512,1024]{1,0:T(8,128)(2,1)S(1)} %bitcast.36), kind=kOutput, calls=%fused_computation | convolution fusion | flops 1074790400 | bytes 4194304 | tf_op jit(solution)/shard_map/dot_general | solution.py:176
  145.4 14.9 %all_to_all.43 = bf16[16,4,32,128]{3,2,1,0:T(8,128)(2,1)S(1)} all-to-all(bf16[16,4,32,128]{3,2,1,0:T(8,128)(2,1)S(1)} %add_convert_fusion), channel_id=1, replica_groups=mesh['x'=4,'z'=16,'y'=4,'c'=2] {'x','y'}, dimensions={0} | all-to-all | bytes 1048576 | tf_op jit(solution)/shard_map/all_to_all | solution.py:178
  160.4 16.6 %all_to_all.44 = bf16[16,32,128]{2,1,0:T(8,128)(2,1)S(1)} all-to-all(bf16[16,32,128]{2,1,0:T(8,128)(2,1)S(1)} %bitcast.41), channel_id=1, replica_groups=mesh['x'=4,'z'=16,'y'=4,'c'=2] {'z'}, dimensions={0} | all-to-all | bytes 262144 | tf_op jit(solution)/shard_map/all_to_all | solution.py:180
  (41 shorter events, 4.2 us)
Async XLA Ops:
  0.6 47.8 %copy-start.4 = (bf16[1,131072]{1,0:T(2,128)(2,1)S(1)}, bf16[1,131072]{1,0:T(2,128)(2,1)}, u32[]{:S(2)}) copy-start(bf16[1,131072]{1,0:T(2,128)(2,1)} %param.6) | copy-start | bytes 786436
  46.5 4.4 %collective-permute-start = (bf16[16,4,32,128]{3,2,1,0:T(8,128)(2,1)S(1)}, bf16[16,4,32,128]{3,2,1,0:T(8,128)(2,1)S(1)}, u32[]{:S(2)}, u32[]{:S(2)}) collective-permute-start(bf16[16,4,32,128]{3,2,1,0:T(8,128)(2,1)S(1)} %all_to_all.41.here), channel_id=1, source_target_pairs={{0,1},{1,0},{2,3},{3,2},{4,5},{5,4},{6,7},{7,6},{8,9},{9,8},{10,11... | collective-permute-start | bytes 1572872 | tf_op jit(solution)/shard_map/ppermute | solution.py:25
  54.2 1.0 copy-start.1
  55.2 17.7 %collective-permute-start.1 = (f32[128,1024]{1,0:T(8,128)S(1)}, f32[128,1024]{1,0:T(8,128)S(1)}, u32[]{:S(2)}, u32[]{:S(2)}) collective-permute-start(f32[128,1024]{1,0:T(8,128)S(1)} %get-tuple-element.20), channel_id=1, source_target_pairs={{0,256},{128,384},{256,0},{384,128},{1,257},{129,385},{257,1},{385... | collective-permute-start | bytes 1572872 | tf_op jit(solution)/shard_map/ppermute | solution.py:25
  58.3 28.0 %all-to-all-start.2 = ((bf16[128,2,512]{2,1,0:T(2,128)(2,1)}), bf16[128,2,512]{2,1,0:T(2,128)(2,1)S(1)}, u32[]{:S(2)}, u32[]{:S(2)}) async-start(bf16[128,2,512]{2,1,0:T(2,128)(2,1)} %reshape.46), calls=%async_computation.2 | async-start | bytes 524288 | tf_op jit(solution)/shard_map/all_to_all | solution.py:152
  66.2 17.3 %collective-permute-start.2 = (f32[128,1024]{1,0:T(8,128)S(1)}, f32[128,1024]{1,0:T(8,128)S(1)}, u32[]{:S(2)}, u32[]{:S(2)}) collective-permute-start(f32[128,1024]{1,0:T(8,128)S(1)} %get-tuple-element.21), channel_id=1, source_target_pairs={{0,128},{128,256},{256,384},{384,0},{1,129},{129,257},{257,385},{3... | collective-permute-start | bytes 1572872 | tf_op jit(solution)/shard_map/ppermute | solution.py:25
  69.9 16.3 %collective-permute-start.3 = (f32[128,1024]{1,0:T(8,128)S(1)}, f32[128,1024]{1,0:T(8,128)S(1)}, u32[]{:S(2)}, u32[]{:S(2)}) collective-permute-start(f32[128,1024]{1,0:T(8,128)S(1)} %get-tuple-element.22), channel_id=1, source_target_pairs={{0,384},{128,0},{256,128},{384,256},{1,385},{129,1},{257,129},{385... | collective-permute-start | bytes 1572872 | tf_op jit(solution)/shard_map/ppermute | solution.py:25
  72.9 19.8 %copy-start.6 = (s32[128]{0:T(128)S(1)}, s32[128]{0:T(128)}, u32[]{:S(2)}) copy-start(s32[128]{0:T(128)} %param.9) | copy-start | bytes 1540
  73.0 49.4 %copy-start.5 = (s32[128]{0:T(128)S(1)}, s32[128]{0:T(128)}, u32[]{:S(2)}) copy-start(s32[128]{0:T(128)} %param.8) | copy-start | bytes 1540
  87.3 10.8 %all-to-all-start.3 = ((f32[8,3,128]{2,1,0:T(4,128)}), f32[8,3,128]{2,1,0:T(4,128)S(1)}, u32[]{:S(2)}, u32[]{:S(2)}) async-start(f32[8,3,128]{2,1,0:T(4,128)} %broadcast_in_dim.15), calls=%async_computation.3 | async-start | bytes 32768 | tf_op jit(solution)/shard_map/all_to_all | solution.py:30
  98.8 23.5 %all-to-all-start.4 = ((f32[16,3,128]{2,1,0:T(4,128)}), f32[16,3,128]{2,1,0:T(4,128)S(1)}, u32[]{:S(2)}, u32[]{:S(2)}) async-start(f32[16,3,128]{2,1,0:T(4,128)} %broadcast_in_dim.16), calls=%async_computation.4 | async-start | bytes 65536 | tf_op jit(solution)/shard_map/all_to_all | solution.py:30
  122.4 16.5 %copy-start = (bf16[1024,1024]{1,0:T(8,128)(2,1)S(1)}, bf16[1024,1024]{1,0:T(8,128)(2,1)}, u32[]{:S(2)}) copy-start(bf16[1024,1024]{1,0:T(8,128)(2,1)} %head.3) | copy-start | bytes 6291460
  122.7 18.0 %copy-start.3 = (bf16[128,1024]{1,0:T(8,128)(2,1)}, bf16[128,1024]{1,0:T(8,128)(2,1)S(1)}, u32[]{:S(2)}) copy-start(bf16[128,1024]{1,0:T(8,128)(2,1)S(1)} %multiply_convert_fusion) | copy-start | bytes 786436
  138.9 3.8 %copy-start.2 = (bf16[1024,512]{1,0:T(8,128)(2,1)S(1)}, bf16[1024,512]{1,0:T(8,128)(2,1)}, u32[]{:S(2)}) copy-start(bf16[1024,512]{1,0:T(8,128)(2,1)} %copy-done.1) | copy-start | bytes 3145732
  140.7 4.5 %collective-permute-start.4 = (bf16[16,4,32,128]{3,2,1,0:T(8,128)(2,1)S(1)}, bf16[16,4,32,128]{3,2,1,0:T(8,128)(2,1)S(1)}, u32[]{:S(2)}, u32[]{:S(2)}) collective-permute-start(bf16[16,4,32,128]{3,2,1,0:T(8,128)(2,1)S(1)} %get-tuple-element.25), channel_id=1, source_target_pairs={{0,1},{1,0},{2,3},{3,2},{4,5},{5,4},{6,7},{7,6},{8,9},{9,8},{10,11... | collective-permute-start | bytes 1572872 | tf_op jit(solution)/shard_map/ppermute | solution.py:25

commit v4 on v3

--- a/solution.py
+++ b/solution.py
@@ -88,22 +88,22 @@
     )(place, here, there, head)
 
 
-def add_kernel(own, far, total):
-    total[...] = own[...] + far[...]
+def add_kernel(own, far, down, total):
+    total[...] = own[...] + far[...] + down[...]
 
 
-def add_far(own, far):
+def add_far(own, far, down):
     rows = pl.BlockSpec((TOK // 2, COLS), lambda i: (i, 0))
     return pl.pallas_call(
         add_kernel,
         out_shape=jax.ShapeDtypeStruct((TOK, COLS), f32),
         grid=(2,),
-        in_specs=[rows, rows],
+        in_specs=[rows] * 3,
         out_specs=rows,
         compiler_params=pltpu.CompilerParams(vmem_limit_bytes=LIMIT),
         cost_estimate=pl.CostEstimate(flops=ADD_COST, bytes_accessed=3 << 19, transcendentals=0),
         name="add_far",
-    )(own, far)
+    )(own, far, down)
 
 
 def feature_kernel(place, grads, head, sent, kept):
@@ -145,12 +145,12 @@
 def local(hidden_states, teacher_logprob, head_weight, token_ids, padding_mask):
     place = jnp.stack([lax.axis_index("x"), lax.axis_index("c")]).astype(jnp.int32)
     here, there = gather_hidden(hidden_states)
-    teacher = teacher_logprob.reshape(Z * Y * C, 2, COLS // 2)
+    teacher = teacher_logprob.reshape(Z * Y * C, 8, COLS // 8)
     teacher, there = lax.optimization_barrier((teacher, there))
     far, up, down, own, hidden_t = partial_logits(place, here, there, head_weight)
     teacher, own = lax.optimization_barrier((teacher, own))
     teacher = lax.all_to_all(teacher, ("z", "y", "c"), 0, 0, tiled=True).reshape(TOK, COLS)
-    logits = add_far(own, shift(far, "x", X, 2)) + (shift(up, "x", X, 1) + shift(down, "x", X, 3))
+    logits = add_far(own, shift(far, "x", X, 2), shift(down, "x", X, 3)) + shift(up, "x", X, 1)
     gap = logits - teacher.astype(f32)
     top = jnp.max(logits, axis=1)
     expo = jnp.exp(logits - top[:, None])

time: 179 us -> 179 us (level)
  starting transfers between devices: 37.1 us -> 33.7 us
  waiting for transfers between devices: 31.9 us -> 33.7 us
  blocking collectives: 92.5 us -> 94.3 us
    all_to_all x1, waiting for transfers between devices: 0.01 us -> 4.64 us  [local(): lax.all_to_all(teacher, ('z', 'y', 'c'), 0, 0, tiled=True)]
    all_to_all x2, starting transfers between devices: 16.3 us -> 11.7 us  [spread(): return lax.all_to_all(sent, axes, 0, 0, tiled=True)]
    ppermute x5, waiting for transfers between devices: 14 us -> 11.2 us  [shift(): lax.ppermute(value, axis, [(i, (i + step) % size) for i in range(size)])]
    ppermute x5, starting transfers between devices: 12.8 us -> 14.7 us  [shift(): lax.ppermute(value, axis, [(i, (i + step) % size) for i in range(size)])]
where the time goes in v4:
time: 179 us; the launch traced here: 178 us
  blocking collectives  94.3 us (53%)
  starting transfers between devices  33.7 us (19%)
  waiting for transfers between devices  33.7 us (19%)
  Pallas kernels  5.25 us (3%)
  other arithmetic  4.23 us (2%)
  local copies, waits for them, and re-layouts  3.25 us (2%)
  matrix products  2.57 us (1%)
    all_to_all x2, blocking collectives, spread(): return lax.all_to_all(sent, axes, 0, 0, tiled=True)  47.5 us
    all_to_all x2, waiting for transfers between devices, spread(): return lax.all_to_all(sent, axes, 0, 0, tiled=True)  17.9 us
    all_to_all x1, blocking collectives, local(): line = lax.all_to_all(plane.reshape(Z, FEAT, TOK), 'z', 0, 0, tiled=True)  16.6 us
    all_to_all x1, blocking collectives, gather_hidden(): lax.all_to_all(sent.reshape(X * Y, K, FEAT, TOK), ('x', 'y'), 0, 0, tiled...  15.3 us
    all_to_all x1, blocking collectives, local(): plane = lax.all_to_all(pair, ('x', 'y'), 0, 0, tiled=True)  14.9 us
    ppermute x5, starting transfers between devices, shift(): lax.ppermute(value, axis, [(i, (i + step) % size) for i in range(size)])  14.7 us
    all_to_all x2, starting transfers between devices, spread(): return lax.all_to_all(sent, axes, 0, 0, tiled=True)  11.7 us
    ppermute x5, waiting for transfers between devices, shift(): lax.ppermute(value, axis, [(i, (i + step) % size) for i in range(size)])  11.2 us
  transfers between devices with their start and end apart: 8, of which 5 were waited for; matrix products, arithmetic and copies ran while one was open for 3% of the time, Pallas kernels for 0%

profile of v4, /device:TPU:6, one launch (start us, length us, event | category | flops | bytes accessed | tf_op | source)
XLA Modules:
  0.0 177.8 jit_solution(1806892332214569970)
XLA Ops:
  0.6 0.8 broadcast_in_dim.12
  1.4 29.7 %all_to_all.40 = bf16[16,32,128]{2,1,0:T(8,128)(2,1)S(1)} all-to-all(bf16[16,32,128]{2,1,0:T(8,128)(2,1)S(1)} %broadcast_in_dim.12), channel_id=1, replica_groups=mesh['x'=4,'z'=16,'y'=4,'c'=2] {'z'}, dimensions={0} | all-to-all | bytes 262144 | tf_op jit(solution)/shard_map/all_to_all | solution.py:30
  31.2 15.3 %all_to_all.41.here = bf16[16,4,32,128]{3,2,1,0:T(8,128)(2,1)S(1)} all-to-all(bf16[16,4,32,128]{3,2,1,0:T(8,128)(2,1)S(1)} %bitcast.44), channel_id=1, replica_groups=mesh['x'=4,'z'=16,'y'=4,'c'=2] {'x','y'}, dimensions={0} | all-to-all | bytes 1048576 | tf_op jit(solution)/shard_map/all_to_all | solution.py:44
  46.5 1.9 %collective-permute-start = (bf16[16,4,32,128]{3,2,1,0:T(8,128)(2,1)S(1)}, bf16[16,4,32,128]{3,2,1,0:T(8,128)(2,1)S(1)}, u32[]{:S(2)}, u32[]{:S(2)}) collective-permute-start(bf16[16,4,32,128]{3,2,1,0:T(8,128)(2,1)S(1)} %all_to_all.41.here), channel_id=1, source_target_pairs={{0,1},{1,0},{2,3},{3,2},{4,5},{5,4},{6,7},{7,6},{8,9},{9,8},{10,11... | collective-permute-start | bytes 1572872 | tf_op jit(solution)/shard_map/ppermute | solution.py:25
  48.4 2.3 %reduce.3 = bf16[131072]{0:T(1024)(128)(2,1)} reduce(bf16[1,131072]{1,0:T(2,128)(2,1)S(1)} %copy-done.4, bf16[]{:T(256)} %constant.33), dimensions={0}, to_apply=%param.6.reduce_sub_computation | reduce | bytes 524290 | tf_op args[1]
  50.8 3.3 %partial_logits.1 = (f32[128,1024]{1,0:T(8,128)S(1)}, f32[128,1024]{1,0:T(8,128)S(1)}, f32[128,1024]{1,0:T(8,128)S(1)}, f32[128,1024]{1,0:T(8,128)S(1)}, bf16[1024,512]{1,0:T(8,128)(2,1)S(1)}) custom-call(s32[2]{0:T(128)S(1)} %pad_add_fusion.place, bf16[16,4,32,128]{3,2,1,0:T(8,128)(2,1)S(1)} %all_to_all.41.here, ...), custom_call_target="tpu_custom_call" | custom-call | flops 1073741824 | bytes 6291456 | tf_op jit(solution)/shard_map/partial_logits/pallas_call | solution.py:73
  54.2 1.0 copy-done.1
  55.1 3.2 %collective-permute-start.1 = (f32[128,1024]{1,0:T(8,128)S(1)}, f32[128,1024]{1,0:T(8,128)S(1)}, u32[]{:S(2)}, u32[]{:S(2)}) collective-permute-start(f32[128,1024]{1,0:T(8,128)S(1)} %get-tuple-element.20), channel_id=1, source_target_pairs={{0,256},{128,384},{256,0},{384,128},{1,257},{129,385},{257,1},{385... | collective-permute-start | bytes 1572872 | tf_op jit(solution)/shard_map/ppermute | solution.py:25
  58.3 3.6 %collective-permute-start.2 = (f32[128,1024]{1,0:T(8,128)S(1)}, f32[128,1024]{1,0:T(8,128)S(1)}, u32[]{:S(2)}, u32[]{:S(2)}) collective-permute-start(f32[128,1024]{1,0:T(8,128)S(1)} %get-tuple-element.21), channel_id=1, source_target_pairs={{0,384},{128,0},{256,128},{384,256},{1,385},{129,1},{257,129},{385... | collective-permute-start | bytes 1572872 | tf_op jit(solution)/shard_map/ppermute | solution.py:25
  61.9 7.3 %all-to-all-start.2 = ((bf16[128,8,128]{2,1,0:T(8,128)(2,1)}), bf16[128,8,128]{2,1,0:T(8,128)(2,1)S(1)}, u32[]{:S(2)}, u32[]{:S(2)}) async-start(bf16[128,8,128]{2,1,0:T(8,128)(2,1)} %bitcast.45), calls=%async_computation.2 | async-start | bytes 524288 | tf_op jit(solution)/shard_map/all_to_all | solution.py:152
  69.3 4.0 %collective-permute-start.3 = (f32[128,1024]{1,0:T(8,128)S(1)}, f32[128,1024]{1,0:T(8,128)S(1)}, u32[]{:S(2)}, u32[]{:S(2)}) collective-permute-start(f32[128,1024]{1,0:T(8,128)S(1)} %get-tuple-element.22), channel_id=1, source_target_pairs={{0,128},{128,256},{256,384},{384,0},{1,129},{129,257},{257,385},{3... | collective-permute-start | bytes 1572872 | tf_op jit(solution)/shard_map/ppermute | solution.py:25
  73.3 10.8 %collective-permute-done.2.down = f32[128,1024]{1,0:T(8,128)S(1)} collective-permute-done((f32[128,1024]{1,0:T(8,128)S(1)}, f32[128,1024]{1,0:T(8,128)S(1)}, u32[]{:S(2)}, u32[]{:S(2)}) %collective-permute-start.2) | collective-permute-done | bytes 524320 | tf_op jit(solution)/shard_map/ppermute | solution.py:25
  84.7 4.6 %all-to-all-done.2 = bf16[128,8,128]{2,1,0:T(8,128)(2,1)S(1)} async-done(((bf16[128,8,128]{2,1,0:T(8,128)(2,1)}), bf16[128,8,128]{2,1,0:T(8,128)(2,1)S(1)}, u32[]{:S(2)}, u32[]{:S(2)}) %all-to-all-start.2) | async-done | bytes 262176 | tf_op jit(solution)/shard_map/all_to_all | solution.py:152
  90.3 5.4 %all-to-all-start.3 = ((f32[8,3,128]{2,1,0:T(4,128)}), f32[8,3,128]{2,1,0:T(4,128)S(1)}, u32[]{:S(2)}, u32[]{:S(2)}) async-start(f32[8,3,128]{2,1,0:T(4,128)} %broadcast_in_dim.15), calls=%async_computation.3 | async-start | bytes 32768 | tf_op jit(solution)/shard_map/all_to_all | solution.py:30
  95.7 5.3 %all-to-all-done.3 = f32[8,3,128]{2,1,0:T(4,128)S(1)} async-done(((f32[8,3,128]{2,1,0:T(4,128)}), f32[8,3,128]{2,1,0:T(4,128)S(1)}, u32[]{:S(2)}, u32[]{:S(2)}) %all-to-all-start.3) | async-done | bytes 12320 | tf_op jit(solution)/shard_map/all_to_all | solution.py:30
  101.8 6.3 %all-to-all-start.4 = ((f32[16,3,128]{2,1,0:T(4,128)}), f32[16,3,128]{2,1,0:T(4,128)S(1)}, u32[]{:S(2)}, u32[]{:S(2)}) async-start(f32[16,3,128]{2,1,0:T(4,128)} %broadcast_in_dim.16), calls=%async_computation.4 | async-start | bytes 65536 | tf_op jit(solution)/shard_map/all_to_all | solution.py:30
  108.1 12.5 %all-to-all-done.4 = f32[16,3,128]{2,1,0:T(4,128)S(1)} async-done(((f32[16,3,128]{2,1,0:T(4,128)}), f32[16,3,128]{2,1,0:T(4,128)S(1)}, u32[]{:S(2)}, u32[]{:S(2)}) %all-to-all-start.4) | async-done | bytes 24608 | tf_op jit(solution)/shard_map/all_to_all | solution.py:30
  121.3 17.8 %all_to_all.42 = bf16[4,128,1024]{2,1,0:T(8,128)(2,1)S(1)} all-to-all(bf16[4,128,1024]{2,1,0:T(8,128)(2,1)S(1)} %broadcast_in_dim.17), channel_id=1, replica_groups=mesh['x'=4,'z'=16,'y'=4,'c'=2] {'x'}, dimensions={0} | all-to-all | bytes 2097152 | tf_op jit(solution)/shard_map/all_to_all | solution.py:30
  139.1 1.8 %feature_parts.1 = (bf16[16,4,32,128]{3,2,1,0:T(8,128)(2,1)S(1)}, f32[16,4,32,128]{3,2,1,0:T(8,128)S(1)}) custom-call(s32[2]{0:T(128)S(1)} %pad_add_fusion.place, bf16[512,1024]{1,0:T(8,128)(2,1)S(1)} %bitcast.42, bf16[1024,1024]{1,0:T(8,128)(2,1)S(1)} %copy-done), custom_call_target="tpu_custom_call" | custom-call | flops 1073741824 | bytes 5242880 | tf_op jit(solution)/shard_map/feature_parts/pallas_call | solution.py:132
  140.9 1.9 %collective-permute-start.4 = (bf16[16,4,32,128]{3,2,1,0:T(8,128)(2,1)S(1)}, bf16[16,4,32,128]{3,2,1,0:T(8,128)(2,1)S(1)}, u32[]{:S(2)}, u32[]{:S(2)}) collective-permute-start(bf16[16,4,32,128]{3,2,1,0:T(8,128)(2,1)S(1)} %get-tuple-element.25), channel_id=1, source_target_pairs={{0,1},{1,0},{2,3},{3,2},{4,5},{5,4},{6,7},{7,6},{8,9},{9,8},{10,11... | collective-permute-start | bytes 1572872 | tf_op jit(solution)/shard_map/ppermute | solution.py:25
  142.8 2.6 %convolution_convert_fusion = bf16[1024,1024]{1,0:T(8,128)(2,1)} fusion(bf16[1024,512]{1,0:T(8,128)(2,1)S(1)} %copy-done.2, bf16[512,1024]{1,0:T(8,128)(2,1)S(1)} %bitcast.43), kind=kOutput, calls=%fused_computation | convolution fusion | flops 1074790400 | bytes 4194304 | tf_op jit(solution)/shard_map/dot_general | solution.py:176
  145.6 14.9 %all_to_all.43 = bf16[16,4,32,128]{3,2,1,0:T(8,128)(2,1)S(1)} all-to-all(bf16[16,4,32,128]{3,2,1,0:T(8,128)(2,1)S(1)} %add_convert_fusion), channel_id=1, replica_groups=mesh['x'=4,'z'=16,'y'=4,'c'=2] {'x','y'}, dimensions={0} | all-to-all | bytes 1048576 | tf_op jit(solution)/shard_map/all_to_all | solution.py:178
  160.6 16.6 %all_to_all.44 = bf16[16,32,128]{2,1,0:T(8,128)(2,1)S(1)} all-to-all(bf16[16,32,128]{2,1,0:T(8,128)(2,1)S(1)} %bitcast.47), channel_id=1, replica_groups=mesh['x'=4,'z'=16,'y'=4,'c'=2] {'z'}, dimensions={0} | all-to-all | bytes 262144 | tf_op jit(solution)/shard_map/all_to_all | solution.py:180
  177.2 0.6 convert_reduce_fusion
  (40 shorter events, 3.3 us)
Async XLA Ops:
  0.6 47.8 %copy-start.4 = (bf16[1,131072]{1,0:T(2,128)(2,1)S(1)}, bf16[1,131072]{1,0:T(2,128)(2,1)}, u32[]{:S(2)}) copy-start(bf16[1,131072]{1,0:T(2,128)(2,1)} %param.6) | copy-start | bytes 786436
  46.5 4.3 %collective-permute-start = (bf16[16,4,32,128]{3,2,1,0:T(8,128)(2,1)S(1)}, bf16[16,4,32,128]{3,2,1,0:T(8,128)(2,1)S(1)}, u32[]{:S(2)}, u32[]{:S(2)}) collective-permute-start(bf16[16,4,32,128]{3,2,1,0:T(8,128)(2,1)S(1)} %all_to_all.41.here), channel_id=1, source_target_pairs={{0,1},{1,0},{2,3},{3,2},{4,5},{5,4},{6,7},{7,6},{8,9},{9,8},{10,11... | collective-permute-start | bytes 1572872 | tf_op jit(solution)/shard_map/ppermute | solution.py:25
  54.2 1.0 copy-start.1
  55.1 18.2 %collective-permute-start.1 = (f32[128,1024]{1,0:T(8,128)S(1)}, f32[128,1024]{1,0:T(8,128)S(1)}, u32[]{:S(2)}, u32[]{:S(2)}) collective-permute-start(f32[128,1024]{1,0:T(8,128)S(1)} %get-tuple-element.20), channel_id=1, source_target_pairs={{0,256},{128,384},{256,0},{384,128},{1,257},{129,385},{257,1},{385... | collective-permute-start | bytes 1572872 | tf_op jit(solution)/shard_map/ppermute | solution.py:25
  58.3 25.8 %collective-permute-start.2 = (f32[128,1024]{1,0:T(8,128)S(1)}, f32[128,1024]{1,0:T(8,128)S(1)}, u32[]{:S(2)}, u32[]{:S(2)}) collective-permute-start(f32[128,1024]{1,0:T(8,128)S(1)} %get-tuple-element.21), channel_id=1, source_target_pairs={{0,384},{128,0},{256,128},{384,256},{1,385},{129,1},{257,129},{385... | collective-permute-start | bytes 1572872 | tf_op jit(solution)/shard_map/ppermute | solution.py:25
  61.9 27.4 %all-to-all-start.2 = ((bf16[128,8,128]{2,1,0:T(8,128)(2,1)}), bf16[128,8,128]{2,1,0:T(8,128)(2,1)S(1)}, u32[]{:S(2)}, u32[]{:S(2)}) async-start(bf16[128,8,128]{2,1,0:T(8,128)(2,1)} %bitcast.45), calls=%async_computation.2 | async-start | bytes 524288 | tf_op jit(solution)/shard_map/all_to_all | solution.py:152
  69.3 15.3 %collective-permute-start.3 = (f32[128,1024]{1,0:T(8,128)S(1)}, f32[128,1024]{1,0:T(8,128)S(1)}, u32[]{:S(2)}, u32[]{:S(2)}) collective-permute-start(f32[128,1024]{1,0:T(8,128)S(1)} %get-tuple-element.22), channel_id=1, source_target_pairs={{0,128},{128,256},{256,384},{384,0},{1,129},{129,257},{257,385},{3... | collective-permute-start | bytes 1572872 | tf_op jit(solution)/shard_map/ppermute | solution.py:25
  84.2 11.5 %copy-start.6 = (s32[128]{0:T(128)S(1)}, s32[128]{0:T(128)}, u32[]{:S(2)}) copy-start(s32[128]{0:T(128)} %param.9) | copy-start | bytes 1540
  84.2 36.5 %copy-start.5 = (s32[128]{0:T(128)S(1)}, s32[128]{0:T(128)}, u32[]{:S(2)}) copy-start(s32[128]{0:T(128)} %param.8) | copy-start | bytes 1540
  90.3 10.8 %all-to-all-start.3 = ((f32[8,3,128]{2,1,0:T(4,128)}), f32[8,3,128]{2,1,0:T(4,128)S(1)}, u32[]{:S(2)}, u32[]{:S(2)}) async-start(f32[8,3,128]{2,1,0:T(4,128)} %broadcast_in_dim.15), calls=%async_computation.3 | async-start | bytes 32768 | tf_op jit(solution)/shard_map/all_to_all | solution.py:30
  101.8 18.9 %all-to-all-start.4 = ((f32[16,3,128]{2,1,0:T(4,128)}), f32[16,3,128]{2,1,0:T(4,128)S(1)}, u32[]{:S(2)}, u32[]{:S(2)}) async-start(f32[16,3,128]{2,1,0:T(4,128)} %broadcast_in_dim.16), calls=%async_computation.4 | async-start | bytes 65536 | tf_op jit(solution)/shard_map/all_to_all | solution.py:30
  120.7 18.3 %copy-start = (bf16[1024,1024]{1,0:T(8,128)(2,1)S(1)}, bf16[1024,1024]{1,0:T(8,128)(2,1)}, u32[]{:S(2)}) copy-start(bf16[1024,1024]{1,0:T(8,128)(2,1)} %head.3) | copy-start | bytes 6291460
  121.1 19.8 %copy-start.3 = (bf16[128,1024]{1,0:T(8,128)(2,1)}, bf16[128,1024]{1,0:T(8,128)(2,1)S(1)}, u32[]{:S(2)}) copy-start(bf16[128,1024]{1,0:T(8,128)(2,1)S(1)} %multiply_convert_fusion) | copy-start | bytes 786436
  139.1 3.8 %copy-start.2 = (bf16[1024,512]{1,0:T(8,128)(2,1)S(1)}, bf16[1024,512]{1,0:T(8,128)(2,1)}, u32[]{:S(2)}) copy-start(bf16[1024,512]{1,0:T(8,128)(2,1)} %copy-done.1) | copy-start | bytes 3145732
  140.9 4.5 %collective-permute-start.4 = (bf16[16,4,32,128]{3,2,1,0:T(8,128)(2,1)S(1)}, bf16[16,4,32,128]{3,2,1,0:T(8,128)(2,1)S(1)}, u32[]{:S(2)}, u32[]{:S(2)}) collective-permute-start(bf16[16,4,32,128]{3,2,1,0:T(8,128)(2,1)S(1)} %get-tuple-element.25), channel_id=1, source_target_pairs={{0,1},{1,0},{2,3},{3,2},{4,5},{5,4},{6,7},{7,6},{8,9},{9,8},{10,11... | collective-permute-start | bytes 1572872 | tf_op jit(solution)/shard_map/ppermute | solution.py:25

commit v5 on v3

--- a/solution.py
+++ b/solution.py
@@ -145,7 +145,7 @@
 def local(hidden_states, teacher_logprob, head_weight, token_ids, padding_mask):
     place = jnp.stack([lax.axis_index("x"), lax.axis_index("c")]).astype(jnp.int32)
     here, there = gather_hidden(hidden_states)
-    teacher = teacher_logprob.reshape(Z * Y * C, 2, COLS // 2)
+    teacher = teacher_logprob.reshape(Z * Y * C, 8, COLS // 8)
     teacher, there = lax.optimization_barrier((teacher, there))
     far, up, down, own, hidden_t = partial_logits(place, here, there, head_weight)
     teacher, own = lax.optimization_barrier((teacher, own))

time: 179 us -> 179 us (level)
  no operation moved by 1% of the time
where the time goes in v5:
time: 179 us; the launch traced here: 178 us
  blocking collectives  92.5 us (52%)
  starting transfers between devices  37.1 us (21%)
  waiting for transfers between devices  31.9 us (18%)
  Pallas kernels  5.2 us (3%)
  other arithmetic  4.15 us (2%)
  local copies, waits for them, and re-layouts  3.24 us (2%)
  matrix products  2.57 us (1%)
    all_to_all x2, blocking collectives, spread(): return lax.all_to_all(sent, axes, 0, 0, tiled=True)  45.8 us
    all_to_all x2, waiting for transfers between devices, spread(): return lax.all_to_all(sent, axes, 0, 0, tiled=True)  17.9 us
    all_to_all x1, blocking collectives, local(): line = lax.all_to_all(plane.reshape(Z, FEAT, TOK), 'z', 0, 0, tiled=True)  16.6 us
    all_to_all x2, starting transfers between devices, spread(): return lax.all_to_all(sent, axes, 0, 0, tiled=True)  16.3 us
    all_to_all x1, blocking collectives, gather_hidden(): lax.all_to_all(sent.reshape(X * Y, K, FEAT, TOK), ('x', 'y'), 0, 0, tiled...  15.3 us
    all_to_all x1, blocking collectives, local(): plane = lax.all_to_all(pair, ('x', 'y'), 0, 0, tiled=True)  14.9 us
    ppermute x5, waiting for transfers between devices, shift(): lax.ppermute(value, axis, [(i, (i + step) % size) for i in range(size)])  14 us
    ppermute x5, starting transfers between devices, shift(): lax.ppermute(value, axis, [(i, (i + step) % size) for i in range(size)])  12.9 us
  transfers between devices with their start and end apart: 8, of which 5 were waited for; matrix products, arithmetic and copies ran while one was open for 3% of the time, Pallas kernels for 0%

profile of v5, /device:TPU:6, one launch (start us, length us, event | category | flops | bytes accessed | tf_op | source)
XLA Modules:
  0.0 177.6 jit_solution(18347847004598234095)
XLA Ops:
  0.6 0.8 broadcast_in_dim.12
  1.4 29.7 %all_to_all.40 = bf16[16,32,128]{2,1,0:T(8,128)(2,1)S(1)} all-to-all(bf16[16,32,128]{2,1,0:T(8,128)(2,1)S(1)} %broadcast_in_dim.12), channel_id=1, replica_groups=mesh['x'=4,'z'=16,'y'=4,'c'=2] {'z'}, dimensions={0} | all-to-all | bytes 262144 | tf_op jit(solution)/shard_map/all_to_all | solution.py:30
  31.2 15.3 %all_to_all.41.here = bf16[16,4,32,128]{3,2,1,0:T(8,128)(2,1)S(1)} all-to-all(bf16[16,4,32,128]{3,2,1,0:T(8,128)(2,1)S(1)} %bitcast.44), channel_id=1, replica_groups=mesh['x'=4,'z'=16,'y'=4,'c'=2] {'x','y'}, dimensions={0} | all-to-all | bytes 1048576 | tf_op jit(solution)/shard_map/all_to_all | solution.py:44
  46.5 1.9 %collective-permute-start = (bf16[16,4,32,128]{3,2,1,0:T(8,128)(2,1)S(1)}, bf16[16,4,32,128]{3,2,1,0:T(8,128)(2,1)S(1)}, u32[]{:S(2)}, u32[]{:S(2)}) collective-permute-start(bf16[16,4,32,128]{3,2,1,0:T(8,128)(2,1)S(1)} %all_to_all.41.here), channel_id=1, source_target_pairs={{0,1},{1,0},{2,3},{3,2},{4,5},{5,4},{6,7},{7,6},{8,9},{9,8},{10,11... | collective-permute-start | bytes 1572872 | tf_op jit(solution)/shard_map/ppermute | solution.py:25
  48.4 2.3 %reduce.3 = bf16[131072]{0:T(1024)(128)(2,1)} reduce(bf16[1,131072]{1,0:T(2,128)(2,1)S(1)} %copy-done.4, bf16[]{:T(256)} %constant.33), dimensions={0}, to_apply=%param.6.reduce_sub_computation | reduce | bytes 524290 | tf_op args[1]
  50.8 3.3 %partial_logits.1 = (f32[128,1024]{1,0:T(8,128)S(1)}, f32[128,1024]{1,0:T(8,128)S(1)}, f32[128,1024]{1,0:T(8,128)S(1)}, f32[128,1024]{1,0:T(8,128)S(1)}, bf16[1024,512]{1,0:T(8,128)(2,1)S(1)}) custom-call(s32[2]{0:T(128)S(1)} %pad_add_fusion.place, bf16[16,4,32,128]{3,2,1,0:T(8,128)(2,1)S(1)} %all_to_all.41.here, ...), custom_call_target="tpu_custom_call" | custom-call | flops 1073741824 | bytes 6291456 | tf_op jit(solution)/shard_map/partial_logits/pallas_call | solution.py:73
  54.1 1.0 copy-done.1
  55.0 3.2 %collective-permute-start.1 = (f32[128,1024]{1,0:T(8,128)S(1)}, f32[128,1024]{1,0:T(8,128)S(1)}, u32[]{:S(2)}, u32[]{:S(2)}) collective-permute-start(f32[128,1024]{1,0:T(8,128)S(1)} %get-tuple-element.20), channel_id=1, source_target_pairs={{0,256},{128,384},{256,0},{384,128},{1,257},{129,385},{257,1},{385... | collective-permute-start | bytes 1572872 | tf_op jit(solution)/shard_map/ppermute | solution.py:25
  58.2 7.9 %all-to-all-start.2 = ((bf16[128,8,128]{2,1,0:T(8,128)(2,1)}), bf16[128,8,128]{2,1,0:T(8,128)(2,1)S(1)}, u32[]{:S(2)}, u32[]{:S(2)}) async-start(bf16[128,8,128]{2,1,0:T(8,128)(2,1)} %bitcast.21), calls=%async_computation.2 | async-start | bytes 524288 | tf_op jit(solution)/shard_map/all_to_all | solution.py:152
  66.1 3.7 %collective-permute-start.2 = (f32[128,1024]{1,0:T(8,128)S(1)}, f32[128,1024]{1,0:T(8,128)S(1)}, u32[]{:S(2)}, u32[]{:S(2)}) collective-permute-start(f32[128,1024]{1,0:T(8,128)S(1)} %get-tuple-element.21), channel_id=1, source_target_pairs={{0,128},{128,256},{256,384},{384,0},{1,129},{129,257},{257,385},{3... | collective-permute-start | bytes 1572872 | tf_op jit(solution)/shard_map/ppermute | solution.py:25
  69.8 2.2 %collective-permute-start.3 = (f32[128,1024]{1,0:T(8,128)S(1)}, f32[128,1024]{1,0:T(8,128)S(1)}, u32[]{:S(2)}, u32[]{:S(2)}) collective-permute-start(f32[128,1024]{1,0:T(8,128)S(1)} %get-tuple-element.22), channel_id=1, source_target_pairs={{0,384},{128,0},{256,128},{384,256},{1,385},{129,1},{257,129},{385... | collective-permute-start | bytes 1572872 | tf_op jit(solution)/shard_map/ppermute | solution.py:25
  72.0 0.8 collective-permute-done.1.far
  72.9 10.6 %collective-permute-done.2 = f32[128,1024]{1,0:T(8,128)S(1)} collective-permute-done((f32[128,1024]{1,0:T(8,128)S(1)}, f32[128,1024]{1,0:T(8,128)S(1)}, u32[]{:S(2)}, u32[]{:S(2)}) %collective-permute-start.2) | collective-permute-done | bytes 524320 | tf_op jit(solution)/shard_map/ppermute | solution.py:25
  83.4 2.7 %collective-permute-done.3 = f32[128,1024]{1,0:T(8,128)S(1)} collective-permute-done((f32[128,1024]{1,0:T(8,128)S(1)}, f32[128,1024]{1,0:T(8,128)S(1)}, u32[]{:S(2)}, u32[]{:S(2)}) %collective-permute-start.3) | collective-permute-done | bytes 524320 | tf_op jit(solution)/shard_map/ppermute | solution.py:25
  87.2 5.4 %all-to-all-start.3 = ((f32[8,3,128]{2,1,0:T(4,128)}), f32[8,3,128]{2,1,0:T(4,128)S(1)}, u32[]{:S(2)}, u32[]{:S(2)}) async-start(f32[8,3,128]{2,1,0:T(4,128)} %broadcast_in_dim.15), calls=%async_computation.3 | async-start | bytes 32768 | tf_op jit(solution)/shard_map/all_to_all | solution.py:30
  92.6 5.3 %all-to-all-done.3 = f32[8,3,128]{2,1,0:T(4,128)S(1)} async-done(((f32[8,3,128]{2,1,0:T(4,128)}), f32[8,3,128]{2,1,0:T(4,128)S(1)}, u32[]{:S(2)}, u32[]{:S(2)}) %all-to-all-start.3) | async-done | bytes 12320 | tf_op jit(solution)/shard_map/all_to_all | solution.py:30
  98.7 11.0 %all-to-all-start.4 = ((f32[16,3,128]{2,1,0:T(4,128)}), f32[16,3,128]{2,1,0:T(4,128)S(1)}, u32[]{:S(2)}, u32[]{:S(2)}) async-start(f32[16,3,128]{2,1,0:T(4,128)} %broadcast_in_dim.16), calls=%async_computation.4 | async-start | bytes 65536 | tf_op jit(solution)/shard_map/all_to_all | solution.py:30
  109.6 12.5 %all-to-all-done.4 = f32[16,3,128]{2,1,0:T(4,128)S(1)} async-done(((f32[16,3,128]{2,1,0:T(4,128)}), f32[16,3,128]{2,1,0:T(4,128)S(1)}, u32[]{:S(2)}, u32[]{:S(2)}) %all-to-all-start.4) | async-done | bytes 24608 | tf_op jit(solution)/shard_map/all_to_all | solution.py:30
  122.8 16.1 %all_to_all.42 = bf16[4,128,1024]{2,1,0:T(8,128)(2,1)S(1)} all-to-all(bf16[4,128,1024]{2,1,0:T(8,128)(2,1)S(1)} %broadcast_in_dim.17), channel_id=1, replica_groups=mesh['x'=4,'z'=16,'y'=4,'c'=2] {'x'}, dimensions={0} | all-to-all | bytes 2097152 | tf_op jit(solution)/shard_map/all_to_all | solution.py:30
  138.8 1.8 %feature_parts.1 = (bf16[16,4,32,128]{3,2,1,0:T(8,128)(2,1)S(1)}, f32[16,4,32,128]{3,2,1,0:T(8,128)S(1)}) custom-call(s32[2]{0:T(128)S(1)} %pad_add_fusion.place, bf16[512,1024]{1,0:T(8,128)(2,1)S(1)} %bitcast.42, bf16[1024,1024]{1,0:T(8,128)(2,1)S(1)} %copy-done), custom_call_target="tpu_custom_call" | custom-call | flops 1073741824 | bytes 5242880 | tf_op jit(solution)/shard_map/feature_parts/pallas_call | solution.py:132
  140.7 1.9 %collective-permute-start.4 = (bf16[16,4,32,128]{3,2,1,0:T(8,128)(2,1)S(1)}, bf16[16,4,32,128]{3,2,1,0:T(8,128)(2,1)S(1)}, u32[]{:S(2)}, u32[]{:S(2)}) collective-permute-start(bf16[16,4,32,128]{3,2,1,0:T(8,128)(2,1)S(1)} %get-tuple-element.25), channel_id=1, source_target_pairs={{0,1},{1,0},{2,3},{3,2},{4,5},{5,4},{6,7},{7,6},{8,9},{9,8},{10,11... | collective-permute-start | bytes 1572872 | tf_op jit(solution)/shard_map/ppermute | solution.py:25
  142.6 2.6 %convolution_convert_fusion = bf16[1024,1024]{1,0:T(8,128)(2,1)} fusion(bf16[1024,512]{1,0:T(8,128)(2,1)S(1)} %copy-done.2, bf16[512,1024]{1,0:T(8,128)(2,1)S(1)} %bitcast.43), kind=kOutput, calls=%fused_computation | convolution fusion | flops 1074790400 | bytes 4194304 | tf_op jit(solution)/shard_map/dot_general | solution.py:176
  145.4 14.9 %all_to_all.43 = bf16[16,4,32,128]{3,2,1,0:T(8,128)(2,1)S(1)} all-to-all(bf16[16,4,32,128]{3,2,1,0:T(8,128)(2,1)S(1)} %add_convert_fusion), channel_id=1, replica_groups=mesh['x'=4,'z'=16,'y'=4,'c'=2] {'x','y'}, dimensions={0} | all-to-all | bytes 1048576 | tf_op jit(solution)/shard_map/all_to_all | solution.py:178
  160.4 16.6 %all_to_all.44 = bf16[16,32,128]{2,1,0:T(8,128)(2,1)S(1)} all-to-all(bf16[16,32,128]{2,1,0:T(8,128)(2,1)S(1)} %bitcast.46), channel_id=1, replica_groups=mesh['x'=4,'z'=16,'y'=4,'c'=2] {'z'}, dimensions={0} | all-to-all | bytes 262144 | tf_op jit(solution)/shard_map/all_to_all | solution.py:180
  (40 shorter events, 3.5 us)
Async XLA Ops:
  0.6 47.8 %copy-start.4 = (bf16[1,131072]{1,0:T(2,128)(2,1)S(1)}, bf16[1,131072]{1,0:T(2,128)(2,1)}, u32[]{:S(2)}) copy-start(bf16[1,131072]{1,0:T(2,128)(2,1)} %param.6) | copy-start | bytes 786436
  46.5 4.3 %collective-permute-start = (bf16[16,4,32,128]{3,2,1,0:T(8,128)(2,1)S(1)}, bf16[16,4,32,128]{3,2,1,0:T(8,128)(2,1)S(1)}, u32[]{:S(2)}, u32[]{:S(2)}) collective-permute-start(bf16[16,4,32,128]{3,2,1,0:T(8,128)(2,1)S(1)} %all_to_all.41.here), channel_id=1, source_target_pairs={{0,1},{1,0},{2,3},{3,2},{4,5},{5,4},{6,7},{7,6},{8,9},{9,8},{10,11... | collective-permute-start | bytes 1572872 | tf_op jit(solution)/shard_map/ppermute | solution.py:25
  54.1 1.0 copy-start.1
  55.0 17.7 %collective-permute-start.1 = (f32[128,1024]{1,0:T(8,128)S(1)}, f32[128,1024]{1,0:T(8,128)S(1)}, u32[]{:S(2)}, u32[]{:S(2)}) collective-permute-start(f32[128,1024]{1,0:T(8,128)S(1)} %get-tuple-element.20), channel_id=1, source_target_pairs={{0,256},{128,384},{256,0},{384,128},{1,257},{129,385},{257,1},{385... | collective-permute-start | bytes 1572872 | tf_op jit(solution)/shard_map/ppermute | solution.py:25
  58.2 28.0 %all-to-all-start.2 = ((bf16[128,8,128]{2,1,0:T(8,128)(2,1)}), bf16[128,8,128]{2,1,0:T(8,128)(2,1)S(1)}, u32[]{:S(2)}, u32[]{:S(2)}) async-start(bf16[128,8,128]{2,1,0:T(8,128)(2,1)} %bitcast.21), calls=%async_computation.2 | async-start | bytes 524288 | tf_op jit(solution)/shard_map/all_to_all | solution.py:152
  66.1 17.3 %collective-permute-start.2 = (f32[128,1024]{1,0:T(8,128)S(1)}, f32[128,1024]{1,0:T(8,128)S(1)}, u32[]{:S(2)}, u32[]{:S(2)}) collective-permute-start(f32[128,1024]{1,0:T(8,128)S(1)} %get-tuple-element.21), channel_id=1, source_target_pairs={{0,128},{128,256},{256,384},{384,0},{1,129},{129,257},{257,385},{3... | collective-permute-start | bytes 1572872 | tf_op jit(solution)/shard_map/ppermute | solution.py:25
  69.8 16.3 %collective-permute-start.3 = (f32[128,1024]{1,0:T(8,128)S(1)}, f32[128,1024]{1,0:T(8,128)S(1)}, u32[]{:S(2)}, u32[]{:S(2)}) collective-permute-start(f32[128,1024]{1,0:T(8,128)S(1)} %get-tuple-element.22), channel_id=1, source_target_pairs={{0,384},{128,0},{256,128},{384,256},{1,385},{129,1},{257,129},{385... | collective-permute-start | bytes 1572872 | tf_op jit(solution)/shard_map/ppermute | solution.py:25
  72.8 19.8 %copy-start.6 = (s32[128]{0:T(128)S(1)}, s32[128]{0:T(128)}, u32[]{:S(2)}) copy-start(s32[128]{0:T(128)} %param.9) | copy-start | bytes 1540
  72.9 49.4 %copy-start.5 = (s32[128]{0:T(128)S(1)}, s32[128]{0:T(128)}, u32[]{:S(2)}) copy-start(s32[128]{0:T(128)} %param.8) | copy-start | bytes 1540
  87.2 10.8 %all-to-all-start.3 = ((f32[8,3,128]{2,1,0:T(4,128)}), f32[8,3,128]{2,1,0:T(4,128)S(1)}, u32[]{:S(2)}, u32[]{:S(2)}) async-start(f32[8,3,128]{2,1,0:T(4,128)} %broadcast_in_dim.15), calls=%async_computation.3 | async-start | bytes 32768 | tf_op jit(solution)/shard_map/all_to_all | solution.py:30
  98.7 23.5 %all-to-all-start.4 = ((f32[16,3,128]{2,1,0:T(4,128)}), f32[16,3,128]{2,1,0:T(4,128)S(1)}, u32[]{:S(2)}, u32[]{:S(2)}) async-start(f32[16,3,128]{2,1,0:T(4,128)} %broadcast_in_dim.16), calls=%async_computation.4 | async-start | bytes 65536 | tf_op jit(solution)/shard_map/all_to_all | solution.py:30
  122.3 16.6 %copy-start = (bf16[1024,1024]{1,0:T(8,128)(2,1)S(1)}, bf16[1024,1024]{1,0:T(8,128)(2,1)}, u32[]{:S(2)}) copy-start(bf16[1024,1024]{1,0:T(8,128)(2,1)} %head.3) | copy-start | bytes 6291460
  122.6 18.0 %copy-start.3 = (bf16[128,1024]{1,0:T(8,128)(2,1)}, bf16[128,1024]{1,0:T(8,128)(2,1)S(1)}, u32[]{:S(2)}) copy-start(bf16[128,1024]{1,0:T(8,128)(2,1)S(1)} %multiply_convert_fusion) | copy-start | bytes 786436
  138.8 3.8 %copy-start.2 = (bf16[1024,512]{1,0:T(8,128)(2,1)S(1)}, bf16[1024,512]{1,0:T(8,128)(2,1)}, u32[]{:S(2)}) copy-start(bf16[1024,512]{1,0:T(8,128)(2,1)} %copy-done.1) | copy-start | bytes 3145732
  140.7 4.5 %collective-permute-start.4 = (bf16[16,4,32,128]{3,2,1,0:T(8,128)(2,1)S(1)}, bf16[16,4,32,128]{3,2,1,0:T(8,128)(2,1)S(1)}, u32[]{:S(2)}, u32[]{:S(2)}) collective-permute-start(bf16[16,4,32,128]{3,2,1,0:T(8,128)(2,1)S(1)} %get-tuple-element.25), channel_id=1, source_target_pairs={{0,1},{1,0},{2,3},{3,2},{4,5},{5,4},{6,7},{7,6},{8,9},{9,8},{10,11... | collective-permute-start | bytes 1572872 | tf_op jit(solution)/shard_map/ppermute | solution.py:25
